TPU v7x, 32 devices: a whole 2x2x4 slice. The times are simulated.
32 devices in a mesh: dp: 16 (over z, x, core), pair: 2 (over y).
Axes of the slice: x: 2, y: 2, z: 4, core: 2. Of those that a mesh axis runs over, the one named last changes fastest.
Arguments:
- tokens: bfloat16 [2, 4096, 768], P('pair', 'dp'), may hold values from -6 to 6
- cotangent: bfloat16 [2, 4096, 768], P('pair', 'dp'), may hold values from -6 to 6
- lengths: int32 [2, 16, 2], P('pair', 'dp'), may hold values from 1 to 192, 256 in all within a row
- mats: float32 [2, 7077888], P(None, ('dp', 'pair')), may hold values from -1.6329932 to 1.6329932, as said below
- mats_m: float32 [2, 7077888], P(None, ('dp', 'pair')), may hold values from -0.5 to 0.5
- mats_v: float32 [2, 7077888], P(None, ('dp', 'pair')), may hold values from 0.0005 to 0.008
- vecs: float32 [2, 9216], P(None, ('dp', 'pair')), may hold values from -1.2 to 2.2, as said below
- vecs_m: float32 [2, 9216], P(None, ('dp', 'pair')), may hold values from -0.5 to 0.5
- vecs_v: float32 [2, 9216], P(None, ('dp', 'pair')), may hold values from 0.0005 to 0.008
Outputs:
- head_out: bfloat16 [2, 4096, 768], P('pair', 'dp')
- token_grad: float32 [2, 4096, 768], P('pair', 'dp')
- contrastive: float32 [], replicated
- grad_norm: float32 [], replicated
- new_mats: float32 [2, 7077888], P(None, ('dp', 'pair'))
- new_mats_m: float32 [2, 7077888], P(None, ('dp', 'pair'))
- new_mats_v: float32 [2, 7077888], P(None, ('dp', 'pair'))
- new_vecs: float32 [2, 9216], P(None, ('dp', 'pair'))
- new_vecs_m: float32 [2, 9216], P(None, ('dp', 'pair'))
- new_vecs_v: float32 [2, 9216], P(None, ('dp', 'pair'))
Inputs may be any that keep to these rules, and one draw needn't show every extreme that they name: Each row of 2 lengths sums to 256; its longest span has at most 192 tokens. `mats`: Real-valued entries. `vecs`: Real-valued entries.
All inputs are finite; a program needn't handle non-finite values.
Results may differ from a plain program's by a relative error of at most 0.017.
Values may be sent and summed in bfloat16 or wider, within the bound.
No kernel may reach another device: no remote copies, remote signals or barrier semaphores. Data moves between devices by JAX's collectives and lax.ppermute only.
A program may use at most 256 MiB of HBM per device.

v0:
```python
import math

import jax
import jax.numpy as jnp
from jax import lax
from jax.sharding import PartitionSpec as P

D = 768
HEADS = 12
HEAD_DIM = 64
FF = 3072
STEP = 10
PL = 7077888
QL = 9216


norm_epsilon = 1e-12
masked_score = -1000000000.0
beta_one = 0.9
beta_two = 0.999
adam_epsilon = 1e-08
weight_decay = 0.01


def matmul(left_side, right_side):
    return jnp.dot(left_side, right_side, preferred_element_type=jnp.float32)


def inner_rows(left_side, right_side):
    return lax.dot_general(
        left_side, right_side, (((0,), (0,)), ((), ())), preferred_element_type=jnp.float32
    )


def outer_cols(left_side, right_side):
    return lax.dot_general(
        left_side, right_side, (((1,), (1,)), ((), ())), preferred_element_type=jnp.float32
    )


def exact_dot(left_side, right_side):
    return jnp.dot(
        left_side, right_side, precision=lax.Precision.HIGHEST, preferred_element_type=jnp.float32
    )


def layer_norm(resid, gain, shift):
    centred = resid - jnp.mean(resid, axis=-1, keepdims=True)
    spread = jnp.mean(centred * centred, axis=-1, keepdims=True)
    return centred * lax.rsqrt(spread + norm_epsilon) * gain + shift


def gelu_exact(before):
    return jax.nn.gelu(before, approximate=False)


def unpack(mat_row, vec_row):
    edge_one = 3 * D * D
    edge_two = 4 * D * D
    edge_three = edge_two + D * FF
    input_weight = mat_row[:edge_one].reshape(D, 3 * D)
    output_weight = mat_row[edge_one:edge_two].reshape(D, D)
    expand_weight = mat_row[edge_two:edge_three].reshape(D, FF)
    shrink_weight = mat_row[edge_three:].reshape(FF, D)
    vector = vec_row.astype(jnp.float32)
    pieces = []
    cursor = 0
    for piece_len in (D, D, D, D, D, FF, D, D, D):
        pieces.append(vector[cursor : cursor + piece_len])
        cursor = cursor + piece_len
    return (input_weight, output_weight, expand_weight, shrink_weight) + tuple(pieces)


def head_scores(queries, key_rows, same_span):
    row_count = queries.shape[0]
    query_heads = queries.reshape(row_count, HEADS, HEAD_DIM)
    key_heads = key_rows.reshape(row_count, HEADS, HEAD_DIM)
    scores = jnp.einsum(
        "thd,shd->hts", query_heads, key_heads, preferred_element_type=jnp.float32
    ) * HEAD_DIM ** (-0.5)
    return jnp.where(same_span[None, :, :], scores, masked_score)


def layer_forward(params, inputs, same_span):
    (
        input_weight,
        output_weight,
        expand_weight,
        shrink_weight,
        query_bias,
        value_bias,
        output_bias,
        first_gain,
        first_shift,
        expand_bias,
        shrink_bias,
        second_gain,
        second_shift,
    ) = params
    row_count = inputs.shape[0]
    low_input = inputs.astype(jnp.bfloat16)
    joint = matmul(low_input, input_weight)
    queries = (joint[:, :D] + query_bias).astype(jnp.bfloat16)
    key_rows = joint[:, D : 2 * D].astype(jnp.bfloat16)
    values = (joint[:, 2 * D :] + value_bias).astype(jnp.bfloat16)
    scores = head_scores(queries, key_rows, same_span)
    row_max = jnp.max(scores, axis=-1, keepdims=True)
    raised = jnp.exp(scores - row_max)
    summed = jnp.sum(raised, axis=-1, keepdims=True)
    portions = raised / summed
    logsum = row_max + jnp.log(summed)
    value_heads = values.reshape(row_count, HEADS, HEAD_DIM)
    attended = jnp.einsum(
        "hts,shd->thd",
        portions.astype(jnp.bfloat16),
        value_heads,
        preferred_element_type=jnp.float32,
    )
    attended = attended.reshape(row_count, D).astype(jnp.bfloat16)
    resid_one = inputs + (matmul(attended, output_weight) + output_bias)
    hidden = layer_norm(resid_one, first_gain, first_shift)
    low_hidden = hidden.astype(jnp.bfloat16)
    before = matmul(low_hidden, expand_weight) + expand_bias
    activated = gelu_exact(before).astype(jnp.bfloat16)
    resid_two = hidden + (matmul(activated, shrink_weight) + shrink_bias)
    output = layer_norm(resid_two, second_gain, second_shift)
    kept = (
        low_input,
        queries,
        key_rows,
        values,
        logsum,
        attended,
        resid_one,
        low_hidden,
        before,
        activated,
        resid_two,
    )
    return (output, kept)


def layer_backward(params, kept, grad_out, same_span):
    (
        input_weight,
        output_weight,
        expand_weight,
        shrink_weight,
        query_bias,
        value_bias,
        output_bias,
        first_gain,
        first_shift,
        expand_bias,
        shrink_bias,
        second_gain,
        second_shift,
    ) = params
    (
        low_input,
        queries,
        key_rows,
        values,
        logsum,
        attended,
        resid_one,
        low_hidden,
        before,
        activated,
        resid_two,
    ) = kept
    row_count = low_input.shape[0]
    _, norm_pull_two = jax.vjp(layer_norm, resid_two, second_gain, second_shift)
    d_resid_two, d_second_gain, d_second_shift = norm_pull_two(grad_out)
    d_feed = d_resid_two.astype(jnp.bfloat16)
    d_shrink = inner_rows(activated, d_feed)
    d_shrink_bias = jnp.sum(d_feed.astype(jnp.float32), axis=0)
    _, gelu_pull = jax.vjp(gelu_exact, before)
    d_before = gelu_pull(outer_cols(d_feed, shrink_weight))[0].astype(jnp.bfloat16)
    d_expand = inner_rows(low_hidden, d_before)
    d_expand_bias = jnp.sum(d_before.astype(jnp.float32), axis=0)
    d_hidden = d_resid_two + outer_cols(d_before, expand_weight)
    _, norm_pull_one = jax.vjp(layer_norm, resid_one, first_gain, first_shift)
    d_resid_one, d_first_gain, d_first_shift = norm_pull_one(d_hidden)
    d_branch = d_resid_one.astype(jnp.bfloat16)
    d_output = inner_rows(attended, d_branch)
    d_output_bias = jnp.sum(d_branch.astype(jnp.float32), axis=0)
    d_attended = outer_cols(d_branch, output_weight).astype(jnp.bfloat16)
    portions = jnp.exp(head_scores(queries, key_rows, same_span) - logsum)
    query_heads = queries.reshape(row_count, HEADS, HEAD_DIM)
    key_heads = key_rows.reshape(row_count, HEADS, HEAD_DIM)
    value_heads = values.reshape(row_count, HEADS, HEAD_DIM)
    d_att_heads = d_attended.reshape(row_count, HEADS, HEAD_DIM)
    d_portions = jnp.einsum(
        "thd,shd->hts", d_att_heads, value_heads, preferred_element_type=jnp.float32
    )
    d_values = jnp.einsum(
        "hts,thd->shd",
        portions.astype(jnp.bfloat16),
        d_att_heads,
        preferred_element_type=jnp.float32,
    )
    d_values = d_values.reshape(row_count, D).astype(jnp.bfloat16)
    d_scores = portions * (d_portions - jnp.sum(d_portions * portions, axis=-1, keepdims=True))
    d_scores = d_scores.astype(jnp.bfloat16)
    score_scale = HEAD_DIM ** (-0.5)
    d_queries = (
        jnp.einsum("hts,shd->thd", d_scores, key_heads, preferred_element_type=jnp.float32)
        * score_scale
    )
    d_queries = d_queries.reshape(row_count, D).astype(jnp.bfloat16)
    d_keys = (
        jnp.einsum("hts,thd->shd", d_scores, query_heads, preferred_element_type=jnp.float32)
        * score_scale
    )
    d_keys = d_keys.reshape(row_count, D).astype(jnp.bfloat16)
    d_joint = jnp.concatenate([d_queries, d_keys, d_values], axis=1)
    d_input_weight = inner_rows(low_input, d_joint)
    d_query_bias = jnp.sum(d_queries.astype(jnp.float32), axis=0)
    d_value_bias = jnp.sum(d_values.astype(jnp.float32), axis=0)
    d_inputs = d_resid_one + outer_cols(d_joint, input_weight)
    mat_grad = jnp.concatenate(
        [
            d_input_weight.reshape(-1),
            d_output.reshape(-1),
            d_expand.reshape(-1),
            d_shrink.reshape(-1),
        ]
    )
    vec_grad = jnp.concatenate(
        [
            d_query_bias,
            d_value_bias,
            d_output_bias,
            d_first_gain,
            d_first_shift,
            d_expand_bias,
            d_shrink_bias,
            d_second_gain,
            d_second_shift,
        ]
    )
    return (d_inputs, mat_grad, vec_grad)


def contrast_rows(anchors, key_table, anchor_index, span_count, score_scale):
    key_count = key_table.shape[0]
    key_index = jnp.arange(key_count, dtype=jnp.int32)
    scores = outer_cols(anchors, key_table) * score_scale
    scores = jnp.where(anchor_index[:, None] == key_index[None, :], masked_score, scores)
    partner = (
        jnp.bitwise_xor(anchor_index // span_count, 1) * span_count + anchor_index % span_count
    )
    row_max = jnp.max(scores, axis=-1, keepdims=True)
    raised = jnp.exp(scores - row_max)
    summed = jnp.sum(raised, axis=-1, keepdims=True)
    logsum = row_max[:, 0] + jnp.log(summed[:, 0])
    target = key_index[None, :] == partner[:, None]
    positive = jnp.sum(jnp.where(target, scores, 0.0), axis=1)
    grads_low = (raised / summed - target.astype(jnp.float32)).astype(jnp.bfloat16)
    return (grads_low, logsum - positive)


def adamw_update(weight, moment_one, moment_two, gradient, step_rate, decay_rate):
    first_new = beta_one * moment_one + (1.0 - beta_one) * gradient
    second_new = beta_two * moment_two + (1.0 - beta_two) * gradient * gradient
    first_hat = first_new / (1.0 - beta_one**STEP)
    second_hat = second_new / (1.0 - beta_two**STEP)
    weight_new = weight - step_rate * (
        first_hat / (jnp.sqrt(second_hat) + adam_epsilon) + decay_rate * weight
    )
    return (weight_new, first_new, second_new)


def body(tokens, cotangent, lengths, mats, mats_m, mats_v, vecs, vecs_m, vecs_v):
    full_mats, full_vecs = (
        lax.all_gather(mats.astype(jnp.bfloat16), ("dp", "pair"), axis=1, tiled=True),
        lax.all_gather(vecs.astype(jnp.bfloat16), ("dp", "pair"), axis=1, tiled=True),
    )
    layer_one = unpack(full_mats[0], full_vecs[0])
    layer_two = unpack(full_mats[1], full_vecs[1])
    inputs = tokens[0].astype(jnp.float32)
    row_count = inputs.shape[0]
    span_lengths = lengths[0, 0]
    span_count = span_lengths.shape[0]
    positions = jnp.arange(row_count, dtype=jnp.int32)
    starts = jnp.cumsum(span_lengths) - span_lengths
    span_of = jnp.sum((positions[:, None] >= starts[None, :]).astype(jnp.int32), axis=1)
    same_span = span_of[:, None] == span_of[None, :]
    heads_mark = positions[None, :] == starts[:, None]
    is_cls = jnp.any(heads_mark, axis=0)[:, None]
    picker = heads_mark.astype(jnp.float32)
    doc_groups = lax.axis_size("dp")
    early_out, kept_one = layer_forward(layer_one, inputs, same_span)
    cls_rows = exact_dot(picker, early_out)
    mixture = jnp.where(is_cls, early_out, inputs)
    late_out, kept_two = layer_forward(layer_two, mixture, same_span)
    sent_cls = cls_rows.astype(jnp.bfloat16)
    every_cls = lax.all_gather(sent_cls, ("dp", "pair"), axis=0, tiled=True)
    key_count = every_cls.shape[0]
    score_scale = 2.0 / math.sqrt(D)
    offset = lax.axis_index(("dp", "pair")) * span_count
    own_index = offset + jnp.arange(span_count, dtype=jnp.int32)
    grads_low, loss_terms = contrast_rows(sent_cls, every_cls, own_index, span_count, score_scale)
    anchor_part = matmul(grads_low, every_cls) * score_scale
    key_part = lax.psum_scatter(
        inner_rows(grads_low, sent_cls) * score_scale,
        ("dp", "pair"),
        scatter_dimension=0,
        tiled=True,
    )
    cls_grad = anchor_part + key_part
    grad_late = cotangent[0].astype(jnp.float32)
    d_mixture, late_mats, late_vecs = layer_backward(layer_two, kept_two, grad_late, same_span)
    grad_early = jnp.where(is_cls, d_mixture, 0.0) + exact_dot(picker.T, cls_grad)
    d_inputs, early_mats, early_vecs = layer_backward(layer_one, kept_one, grad_early, same_span)
    token_grad = d_inputs + jnp.where(is_cls, 0.0, d_mixture)
    all_pieces = (
        lax.all_to_all(
            early_mats.reshape(doc_groups, -1).astype(jnp.bfloat16),
            "dp",
            split_axis=0,
            concat_axis=0,
            tiled=True,
        ).astype(jnp.float32),
        lax.all_to_all(
            late_mats.reshape(doc_groups, -1).astype(jnp.bfloat16),
            "dp",
            split_axis=0,
            concat_axis=0,
            tiled=True,
        ).astype(jnp.float32),
        lax.all_to_all(
            early_vecs.reshape(doc_groups, -1).astype(jnp.bfloat16),
            "dp",
            split_axis=0,
            concat_axis=0,
            tiled=True,
        ).astype(jnp.float32),
        lax.all_to_all(
            late_vecs.reshape(doc_groups, -1).astype(jnp.bfloat16),
            "dp",
            split_axis=0,
            concat_axis=0,
            tiled=True,
        ).astype(jnp.float32),
    )
    early_mats_part, late_mats_part, early_vecs_part, late_vecs_part = (
        lax.psum_scatter(
            jnp.sum(all_pieces[0], axis=0).astype(jnp.bfloat16),
            "pair",
            scatter_dimension=0,
            tiled=True,
        ).astype(jnp.float32),
        lax.psum_scatter(
            jnp.sum(all_pieces[1], axis=0).astype(jnp.bfloat16),
            "pair",
            scatter_dimension=0,
            tiled=True,
        ).astype(jnp.float32),
        lax.psum_scatter(
            jnp.sum(all_pieces[2], axis=0).astype(jnp.bfloat16),
            "pair",
            scatter_dimension=0,
            tiled=True,
        ).astype(jnp.float32),
        lax.psum_scatter(
            jnp.sum(all_pieces[3], axis=0).astype(jnp.bfloat16),
            "pair",
            scatter_dimension=0,
            tiled=True,
        ).astype(jnp.float32),
    )
    grad_mats = jnp.stack([early_mats_part, late_mats_part])
    grad_vecs = jnp.stack([early_vecs_part, late_vecs_part])
    square_sum = jnp.sum(grad_mats * grad_mats) + jnp.sum(grad_vecs * grad_vecs)
    total_sq, loss_sum = lax.psum((square_sum, jnp.sum(loss_terms)), ("dp", "pair"))
    grad_norm = jnp.sqrt(total_sq)
    clip_factor = jnp.minimum(1.0, math.sqrt(2 * (PL + QL)) / (grad_norm + 1e-06))
    new_mats, new_mats_m, new_mats_v = adamw_update(
        mats, mats_m, mats_v, grad_mats * clip_factor, 0.1, weight_decay
    )
    new_vecs, new_vecs_m, new_vecs_v = adamw_update(
        vecs, vecs_m, vecs_v, grad_vecs * clip_factor, 0.5, 0.0
    )
    contrastive = loss_sum / key_count
    return (
        late_out.astype(jnp.bfloat16)[None],
        token_grad[None],
        contrastive,
        grad_norm,
        new_mats,
        new_mats_m,
        new_mats_v,
        new_vecs,
        new_vecs_m,
        new_vecs_v,
    )


def solution(mesh):
    return jax.shard_map(
        body,
        mesh=mesh,
        in_specs=(
            P("pair", "dp", None),
            P("pair", "dp", None),
            P("pair", "dp", None),
            P(None, ("dp", "pair")),
            P(None, ("dp", "pair")),
            P(None, ("dp", "pair")),
            P(None, ("dp", "pair")),
            P(None, ("dp", "pair")),
            P(None, ("dp", "pair")),
        ),
        out_specs=(
            P("pair", "dp", None),
            P("pair", "dp", None),
            P(),
            P(),
            P(None, ("dp", "pair")),
            P(None, ("dp", "pair")),
            P(None, ("dp", "pair")),
            P(None, ("dp", "pair")),
            P(None, ("dp", "pair")),
            P(None, ("dp", "pair")),
        ),
        check_vma=False,
    )
```

profile of v0, /device:TPU:0, one launch (start us, length us, event | category | flops | bytes accessed | tf_op | source)
XLA Modules:
  0.0 1589.4 jit_solution(8070813884571725863)
XLA Ops:
  9.9 71.6 %all-gather = bf16[32,288,2]{1,2,0:T(2,128)(2,1)S(1)} all-gather(bf16[1,288,2]{1,2,0:T(2,128)(2,1)S(1)} %convert_bitcast_fusion), channel_id=1, replica_groups=mesh['dp'=16,'pair'=2] {'dp','pair'}, dimensions={0}, use_global_device_ids=true | all-gather | bytes 38016 | tf_op jit(solution)/shard_map/all_gather | solution.py:278
  85.8 98.4 %all-gather.4.cloned.1.call-done = bf16[2,7077888]{1,0:T(2,128)(2,1)} async-done(((bf16[2,221184]{1,0:T(2,128)(2,1)}), bf16[2,7077888]{1,0:T(2,128)(2,1)}) %all-gather.4.cloned.1.call-update) | async-done | bytes 28311568 | tf_op jit(solution)/shard_map/all_gather | solution.py:277
  184.1 26.3 %slice_reduce_fusion.6 = (bf16[589824]{0:T(1024)(128)(2,1)S(1)}, bf16[589824]{0:T(1024)(128)(2,1)S(1)}) fusion(bf16[2,7077888]{1,0:T(2,128)(2,1)} %all-gather.4.cloned.1.call-done), kind=kLoop, calls=%fused_computation.68 | loop fusion | bytes 4718592 | tf_op jit(solution)/shard_map/slice | solution.py:62
  214.1 109.5 %slice_reduce_fusion = (bf16[2359296]{0:T(1024)(128)(2,1)}, bf16[2359296]{0:T(1024)(128)(2,1)}, bf16[2359296]{0:T(1024)(128)(2,1)}, bf16[2359296]{0:T(1024)(128)(2,1)}) fusion(bf16[2,7077888]{1,0:T(2,128)(2,1)} %all-gather.4.cloned.1.call-done), kind=kLoop, calls=%fused_computation.2 | loop fusion | bytes 37748736 | tf_op jit(solution)/shard_map/slice | solution.py:64
  332.9 79.0 %slice_reduce_fusion.5 = (bf16[1769472]{0:T(1024)(128)(2,1)}, bf16[1769472]{0:T(1024)(128)(2,1)}) fusion(bf16[2,7077888]{1,0:T(2,128)(2,1)} %all-gather.4.cloned.1.call-done), kind=kLoop, calls=%fused_computation.7 | loop fusion | bytes 14155776 | tf_op jit(solution)/shard_map/slice | solution.py:61
  528.4 65.9 %all-gather.1 = bf16[32,2,768]{2,1,0:T(2,128)(2,1)S(1)} all-gather(bf16[1,2,768]{2,1,0:T(2,128)(2,1)S(1)} %bitcast.183), channel_id=1, replica_groups=mesh['dp'=16,'pair'=2] {'dp','pair'}, dimensions={0}, use_global_device_ids=true | all-gather | bytes 101376 | tf_op jit(solution)/shard_map/all_gather | solution.py:299
  620.2 38.0 %pad_maximum_fusion.1 = bf16[7077888]{0:T(1024)(128)(2,1)} fusion(bf16[2359296]{0:T(1024)(128)(2,1)} %reshape.515, bf16[2359296]{0:T(1024)(128)(2,1)} %bitcast.143, bf16[589824]{0:T(1024)(128)(2,1)} %reshape.513, bf16[1769472]{0:T(1024)(128)(2,1)S(1)} %reshape.512), kind=kLoop, calls=%fused_computation.1 | loop fusion | flops 56623104 | bytes 28311552 | tf_op jit(solution)/shard_map/concatenate | solution.py:222
  658.3 18.9 %convert_element_type.363 = bf16[16,1,442368]{2,1,0:T(2,128)(2,1)} reshape(bf16[7077888]{0:T(1024)(128)(2,1)} %pad_maximum_fusion.1) | data formatting | bytes 28311552 | tf_op jit(solution)/shard_map/convert_element_type | solution.py:327
  677.7 85.2 %reduce.86 = bf16[16,442368]{1,0:T(8,128)(2,1)} reduce(bf16[16,1,442368]{2,1,0:T(2,128)(2,1)} %convert_element_type.363, bf16[]{:T(256)} %broadcast.620), dimensions={1}, to_apply=%convert_element_type.363.reduce_sub_computation | reduce | bytes 28311554 | tf_op jit(solution)/shard_map/convert_element_type | solution.py:327
  763.0 25.2 %reshape.548 = bf16[16,2,221184]{2,1,0:T(2,128)(2,1)} reshape(bf16[16,442368]{1,0:T(8,128)(2,1)} %reduce.86) | data formatting | bytes 28311552
  854.0 37.9 %pad_maximum_fusion = bf16[7077888]{0:T(1024)(128)(2,1)} fusion(bf16[2359296]{0:T(1024)(128)(2,1)} %reshape.511, bf16[2359296]{0:T(1024)(128)(2,1)} %bitcast.142, bf16[589824]{0:T(1024)(128)(2,1)} %reshape.509, bf16[1769472]{0:T(1024)(128)(2,1)S(1)} %reshape.508), kind=kLoop, calls=%fused_computation | loop fusion | flops 56623104 | bytes 28311552 | tf_op jit(solution)/shard_map/concatenate | solution.py:222
  891.9 19.3 %convert_element_type.362 = bf16[16,1,442368]{2,1,0:T(2,128)(2,1)} reshape(bf16[7077888]{0:T(1024)(128)(2,1)} %pad_maximum_fusion) | data formatting | bytes 28311552 | tf_op jit(solution)/shard_map/convert_element_type | solution.py:320
  911.2 85.0 %reduce.87 = bf16[16,442368]{1,0:T(8,128)(2,1)} reduce(bf16[16,1,442368]{2,1,0:T(2,128)(2,1)} %convert_element_type.362, bf16[]{:T(256)} %broadcast.620), dimensions={1}, to_apply=%convert_element_type.362.reduce_sub_computation | reduce | bytes 28311554 | tf_op jit(solution)/shard_map/convert_element_type | solution.py:320
  996.2 25.2 %reshape.550 = bf16[16,2,221184]{2,1,0:T(2,128)(2,1)} reshape(bf16[16,442368]{1,0:T(8,128)(2,1)} %reduce.87) | data formatting | bytes 28311552
  1021.4 23.1 %all-to-all-done.1 = bf16[16,2,221184]{2,1,0:T(2,128)(2,1)} async-done(((bf16[16,2,221184]{2,1,0:T(2,128)(2,1)}), bf16[16,2,221184]{2,1,0:T(2,128)(2,1)}, u32[]{:S(2)}, u32[]{:S(2)}) %all-to-all-start.1) | async-done | bytes 14155808 | tf_op jit(solution)/shard_map/all_to_all | solution.py:326
  1044.4 59.7 %all-to-all-start = ((bf16[16,2,221184]{2,1,0:T(2,128)(2,1)}), bf16[16,2,221184]{2,1,0:T(2,128)(2,1)}, u32[]{:S(2)}, u32[]{:S(2)}) async-start(bf16[16,2,221184]{2,1,0:T(2,128)(2,1)} %reshape.550), calls=%async_computation | async-start | bytes 28311552 | tf_op jit(solution)/shard_map/all_to_all | solution.py:319
  1104.2 22.4 %reshape.549 = bf16[16,1,442368]{2,1,0:T(2,128)(2,1)} reshape(bf16[16,2,221184]{2,1,0:T(2,128)(2,1)} %all-to-all-done.1) | data formatting | bytes 28311552
  1126.6 28.2 %reduce_sum.498 = bf16[442368]{0:T(1024)(128)(2,1)} reduce(bf16[16,1,442368]{2,1,0:T(2,128)(2,1)} %reshape.549, bf16[]{:T(256)} %constant.169.clone.1), dimensions={0,1}, to_apply=%region_33.34 | reduce | flops 6635520 | bytes 15040514 | tf_op jit(solution)/shard_map/reduce_sum | solution.py:356
  1154.9 200.4 %all-to-all-done = bf16[16,2,221184]{2,1,0:T(2,128)(2,1)} async-done(((bf16[16,2,221184]{2,1,0:T(2,128)(2,1)}), bf16[16,2,221184]{2,1,0:T(2,128)(2,1)}, u32[]{:S(2)}, u32[]{:S(2)}) %all-to-all-start) | async-done | bytes 14155808 | tf_op jit(solution)/shard_map/all_to_all | solution.py:319
  1355.3 22.3 %reshape.551 = bf16[16,1,442368]{2,1,0:T(2,128)(2,1)} reshape(bf16[16,2,221184]{2,1,0:T(2,128)(2,1)} %all-to-all-done) | data formatting | bytes 28311552
  1377.7 28.2 %reduce_sum.497 = bf16[442368]{0:T(1024)(128)(2,1)} reduce(bf16[16,1,442368]{2,1,0:T(2,128)(2,1)} %reshape.551, bf16[]{:T(256)} %constant.169.clone.1), dimensions={0,1}, to_apply=%region_31.32 | reduce | flops 6635520 | bytes 15040514 | tf_op jit(solution)/shard_map/reduce_sum | solution.py:350
  1409.7 59.7 %all-to-all-start.3 = ((bf16[16,2,288]{2,1,0:T(2,128)(2,1)}), bf16[16,2,288]{2,1,0:T(2,128)(2,1)S(1)}, u32[]{:S(2)}, u32[]{:S(2)}) async-start(bf16[16,2,288]{2,1,0:T(2,128)(2,1)} %reshape.552), calls=%async_computation.3 | async-start | bytes 49152 | tf_op jit(solution)/shard_map/all_to_all | solution.py:340
  1493.4 22.8 %all-reduce.13.cloned.1.call-done = (bf16[442368]{0:T(1024)(128)(2,1)}, bf16[442368]{0:T(1024)(128)(2,1)}) async-done(((bf16[442368]{0:T(1024)(128)(2,1)}, bf16[442368]{0:T(1024)(128)(2,1)}), (bf16[442368]{0:T(1024)(128)(2,1)}, bf16[442368]{0:T(1024)(128)(2,1)})) %all-reduce.13.cloned.1.call-update) | async-done | bytes 1769488
  1528.7 39.5 %all-reduce.5 = (f32[]{:T(128)}, f32[]{:T(128)}) all-reduce(f32[]{:T(128)} %subtract_reduce_fusion, f32[]{:T(128)S(6)} %add.347), channel_id=1, replica_groups=mesh['dp'=16,'pair'=2] {'dp','pair'}, use_global_device_ids=true, to_apply=%region_30.31 | all-reduce | flops 2 | bytes 16 | tf_op jit(solution)/shard_map/psum | solution.py:377
  (488 shorter events, 275.7 us)
Async XLA Ops:
  7.2 75.7 %copy-start.141 = (s32[1,1,2]{2,1,0:T(1,128)S(1)}, s32[1,1,2]{2,1,0:T(1,128)}, u32[]{:S(2)}) copy-start(s32[1,1,2]{2,1,0:T(1,128)} %param.11) | copy-start | bytes 28
  7.2 176.9 %all-gather.4.cloned.1.call-start = ((), (), s32[]{:S(2)}) async-start(), calls=%async_computation.4 | async-start | bytes 29196288 | tf_op jit(solution)/shard_map/all_gather | solution.py:277
  9.8 783.8 %all-reduce.11.cloned.1.call-start = ((), (), s32[]{:S(2)}) async-start(), calls=%async_computation.5 | async-start | bytes 393216
  85.0 386.9 %copy-start.52 = (f32[768]{0:T(1024)}, f32[768]{0:T(1024)S(1)}, u32[]{:S(2)}) copy-start(f32[768]{0:T(1024)S(1)} %get-tuple-element.128) | copy-start | bytes 9220
  85.0 386.9 %copy-start.57 = (f32[768]{0:T(1024)}, f32[768]{0:T(1024)S(1)}, u32[]{:S(2)}) copy-start(f32[768]{0:T(1024)S(1)} %get-tuple-element.129) | copy-start | bytes 9220
  85.0 390.5 %copy-start.62 = (f32[768]{0:T(1024)}, f32[768]{0:T(1024)S(1)}, u32[]{:S(2)}) copy-start(f32[768]{0:T(1024)S(1)} %get-tuple-element.132) | copy-start | bytes 9220
  85.0 390.5 %copy-start.75 = (f32[768]{0:T(1024)}, f32[768]{0:T(1024)S(1)}, u32[]{:S(2)}) copy-start(f32[768]{0:T(1024)S(1)} %get-tuple-element.131) | copy-start | bytes 9220
  788.3 256.2 %all-to-all-start.1 = ((bf16[16,2,221184]{2,1,0:T(2,128)(2,1)}), bf16[16,2,221184]{2,1,0:T(2,128)(2,1)}, u32[]{:S(2)}, u32[]{:S(2)}) async-start(bf16[16,2,221184]{2,1,0:T(2,128)(2,1)} %reshape.548), calls=%async_computation.1 | async-start | bytes 28311552 | tf_op jit(solution)/shard_map/all_to_all | solution.py:326
  1044.4 310.8 %all-to-all-start = ((bf16[16,2,221184]{2,1,0:T(2,128)(2,1)}), bf16[16,2,221184]{2,1,0:T(2,128)(2,1)}, u32[]{:S(2)}, u32[]{:S(2)}) async-start(bf16[16,2,221184]{2,1,0:T(2,128)(2,1)} %reshape.550), calls=%async_computation | async-start | bytes 28311552 | tf_op jit(solution)/shard_map/all_to_all | solution.py:319
  1104.1 412.0 %all-reduce.13.cloned.1.call-start = ((), (), s32[]{:S(2)}) async-start(), calls=%async_computation.6 | async-start | bytes 3538944
  1377.6 91.8 %copy-start.142 = (u32[32]{0:T(128)S(1)}, u32[32]{0:T(128)}, u32[]{:S(2)}) copy-start(u32[32]{0:T(128)} %constant.199) | copy-start | bytes 388
  1377.6 93.7 %copy-start.92 = (bf16[12,64]{1,0:T(8,128)(2,1)S(1)}, bf16[12,64]{1,0:T(8,128)(2,1)}, u32[]{:S(2)}) copy-start(bf16[12,64]{1,0:T(8,128)(2,1)} %get-tuple-element.123) | copy-start | bytes 4612
  1377.6 94.2 %copy-start.106 = (bf16[768]{0:T(1024)(128)(2,1)S(1)}, bf16[768]{0:T(1024)(128)(2,1)}, u32[]{:S(2)}) copy-start(bf16[768]{0:T(1024)(128)(2,1)} %get-tuple-element.65) | copy-start | bytes 4612
  1377.6 94.4 %copy-start.132 = (bf16[768]{0:T(1024)(128)(2,1)S(1)}, bf16[768]{0:T(1024)(128)(2,1)}, u32[]{:S(2)}) copy-start(bf16[768]{0:T(1024)(128)(2,1)} %get-tuple-element.20) | copy-start | bytes 4612
  1377.6 94.6 %copy-start.131 = (bf16[768]{0:T(1024)(128)(2,1)S(1)}, bf16[768]{0:T(1024)(128)(2,1)}, u32[]{:S(2)}) copy-start(bf16[768]{0:T(1024)(128)(2,1)} %get-tuple-element.27) | copy-start | bytes 4612
  1377.7 94.8 %copy-start.110 = (bf16[3072]{0:T(1024)(128)(2,1)S(1)}, bf16[3072]{0:T(1024)(128)(2,1)}, u32[]{:S(2)}) copy-start(bf16[3072]{0:T(1024)(128)(2,1)} %get-tuple-element.63) | copy-start | bytes 18436
  1377.7 95.1 %copy-start.105 = (bf16[768]{0:T(1024)(128)(2,1)S(1)}, bf16[768]{0:T(1024)(128)(2,1)}, u32[]{:S(2)}) copy-start(bf16[768]{0:T(1024)(128)(2,1)} %get-tuple-element.61) | copy-start | bytes 4612
  1377.7 95.3 %copy-start.108 = (bf16[768]{0:T(1024)(128)(2,1)S(1)}, bf16[768]{0:T(1024)(128)(2,1)}, u32[]{:S(2)}) copy-start(bf16[768]{0:T(1024)(128)(2,1)} %get-tuple-element.18) | copy-start | bytes 4612
  1377.7 95.5 %copy-start.107 = (bf16[768]{0:T(1024)(128)(2,1)S(1)}, bf16[768]{0:T(1024)(128)(2,1)}, u32[]{:S(2)}) copy-start(bf16[768]{0:T(1024)(128)(2,1)} %get-tuple-element.26) | copy-start | bytes 4612
  1377.7 103.2 %copy-start.113 = (f32[2]{0:T(128)S(1)}, f32[2]{0:T(128)}, u32[]{:S(2)}) copy-start(f32[2]{0:T(128)} %copy-done.111) | copy-start | bytes 28
  1377.7 103.2 %copy-start.116 = (f32[2]{0:T(128)S(1)}, f32[2]{0:T(128)}, u32[]{:S(2)}) copy-start(f32[2]{0:T(128)} %copy-done.114) | copy-start | bytes 28
  1377.7 103.2 %copy-start.133 = (f32[2]{0:T(128)S(1)}, f32[2]{0:T(128)}, u32[]{:S(2)}) copy-start(f32[2]{0:T(128)} %get-tuple-element.45) | copy-start | bytes 28
  1409.7 66.2 %all-to-all-start.3 = ((bf16[16,2,288]{2,1,0:T(2,128)(2,1)}), bf16[16,2,288]{2,1,0:T(2,128)(2,1)S(1)}, u32[]{:S(2)}, u32[]{:S(2)}) async-start(bf16[16,2,288]{2,1,0:T(2,128)(2,1)} %reshape.552), calls=%async_computation.3 | async-start | bytes 49152 | tf_op jit(solution)/shard_map/all_to_all | solution.py:340
  1475.9 11.5 all-to-all-start.2
  (134 other events, 1206.7 us)
Sparse Core Ops, SparseCore 0:
  11.5 172.5 all-gather.3
  596.5 119.0 all-reduce.10
  1406.1 109.9 all-reduce.12
where the time goes:
time: 1600 us; the launch traced here: 1590 us
  local copies, waits for them, and re-layouts  478 us (30%)
  waiting for transfers between devices  351 us (22%)
  other arithmetic  335 us (21%)
  blocking collectives  182 us (11%)
  starting transfers between devices  130 us (8%)
  matrix products  90.9 us (6%)
  between operations  22 us (1%)
    all_to_all x1, waiting for transfers between devices, body(): lax.all_to_all(early_mats.reshape(doc_groups, -1).astype(jnp.bfloat16), '...  200 us
    unnamed x335, local copies, waits for them, and re-layouts  121 us
    slice x1, local copies, waits for them, and re-layouts, unpack(): shrink_weight = mat_row[edge_three:].reshape(FF, D)  110 us
    all_gather x1, waiting for transfers between devices, body(): lax.all_gather(mats.astype(jnp.bfloat16), ('dp', 'pair'), axis=1, tiled=T...  98.4 us
    convert_element_type x1, other arithmetic, body(): late_mats.reshape(doc_groups, -1).astype(jnp.bfloat16)  85.2 us
    convert_element_type x1, other arithmetic, body(): early_mats.reshape(doc_groups, -1).astype(jnp.bfloat16)  85 us
    slice x1, local copies, waits for them, and re-layouts, unpack(): input_weight = mat_row[:edge_one].reshape(D, 3 * D)  79 us
    concatenate x2, other arithmetic, layer_backward(): jnp.concatenate([d_input_weight.reshape(-1), d_output.reshape(-1), d_expa...  76 us
  transfers between devices with their start and end apart: 7, of which 6 were waited for; matrix products, arithmetic and copies ran while one was open for 30% of the time, Pallas kernels for 0%

commit v1 on v0

--- a/solution.py
+++ b/solution.py
@@ -3,6 +3,8 @@
 import jax
 import jax.numpy as jnp
 from jax import lax
+from jax.experimental import pallas as pl
+from jax.experimental.pallas import tpu as pltpu
 from jax.sharding import PartitionSpec as P
 
 D = 768
@@ -13,13 +15,812 @@
 PL = 7077888
 QL = 9216
 
-
 norm_epsilon = 1e-12
 masked_score = -1000000000.0
 beta_one = 0.9
 beta_two = 0.999
 adam_epsilon = 1e-08
 weight_decay = 0.01
+
+F32 = jnp.float32
+BF16 = jnp.bfloat16
+TOK = 256
+GRAN = 96
+GRANS = PL // D // GRAN
+VMEM_BYTES = 63_000_000
+
+V_BQ, V_BV, V_BO, V_G1, V_C1, V_B1, V_B2, V_G2, V_C2 = 0, 1, 2, 3, 4, 5, 9, 10, 11
+
+R_E, R_DF, R_H, R_DA, R_ATT, R_DO, R_U, R_DQ, R_Q, R_DATT, R_WK, R_PU = (
+    0, 8, 10, 12, 20, 22, 24, 26, 28, 30, 32, 56,
+)
+PAY = 80
+PAY_A = 48
+
+
+def nn(a, b):
+    return lax.dot_general(a, b, (((1,), (0,)), ((), ())), preferred_element_type=F32)
+
+
+def nt(a, b):
+    return lax.dot_general(a, b, (((1,), (1,)), ((), ())), preferred_element_type=F32)
+
+
+def tn(a, b):
+    return lax.dot_general(a, b, (((0,), (0,)), ((), ())), preferred_element_type=F32)
+
+
+def iota(shape, axis):
+    return lax.broadcasted_iota(jnp.int32, shape, axis)
+
+
+def erf(x):
+    x = jnp.clip(x, -3.832506856900711, 3.832506856900711)
+    s = x * x
+    top = 0.00022905065861350646
+    for c in (0.0034082910107109506, 0.050955695062380861, 0.18520832239976145, 1.128379143519084):
+        top = top * s + c
+    low = -1.1791602954361697e-7
+    for c in (
+        0.000023547966471313185,
+        0.0010179625278914885,
+        0.014070470171167667,
+        0.11098505178285362,
+        0.49746925110067538,
+        1.0,
+    ):
+        low = low * s + c
+    return x * top / low
+
+
+def gelu_both(a):
+    phi = 0.5 + 0.5 * erf(a * math.sqrt(0.5))
+    return a * phi, phi + a * jnp.exp(-0.5 * a * a) * (1.0 / math.sqrt(2.0 * math.pi))
+
+
+def norm_forward(r):
+    centred = r - jnp.mean(r, axis=-1, keepdims=True)
+    rstd = lax.rsqrt(jnp.mean(centred * centred, axis=-1, keepdims=True) + norm_epsilon)
+    return centred * rstd, rstd
+
+
+def norm_backward(dy, gain, xhat, rstd):
+    dx = dy * gain
+    return rstd * (
+        dx - jnp.mean(dx, axis=-1, keepdims=True) - xhat * jnp.mean(dx * xhat, axis=-1, keepdims=True)
+    )
+
+
+def colsum(v):
+    return jnp.sum(v, axis=0, keepdims=True)
+
+
+def flip(v, axis, bit):
+    return lax.ppermute(v, axis, [(i, i ^ bit) for i in range(lax.axis_size(axis))])
+
+
+def core_flip(v):
+    return flip(v, "dp", 1)
+
+
+def x_flip(v):
+    return flip(v, "dp", 2)
+
+
+def y_flip(v):
+    return flip(v, "pair", 1)
+
+
+def z_up(v):
+    n = lax.axis_size("dp")
+    return lax.ppermute(v, "dp", [(i, (i + 4) % n) for i in range(n)])
+
+
+def gather_pieces(own, split):
+    out = []
+    slot = own
+    for k in range(4):
+        cut = split[k]
+        over_x = x_flip(slot)
+        over_y = y_flip(slot)
+        out += [slot, over_x, over_y, y_flip(over_x[:cut]), x_flip(over_y[cut:])]
+        if k < 3:
+            slot = z_up(slot)
+    return out + [core_flip(p) for p in out]
+
+
+def doubled(v, dp, pair):
+    for axis, bit, here in (
+        ("pair", 1, pair),
+        ("dp", 1, dp & 1),
+        ("dp", 2, (dp >> 1) & 1),
+        ("dp", 4, (dp >> 2) & 1),
+        ("dp", 8, (dp >> 3) & 1),
+    ):
+        r = flip(v, axis, bit)
+        v = jnp.where(here == 0, jnp.concatenate([v, r], 0), jnp.concatenate([r, v], 0))
+    return v
+
+
+def summed(v):
+    for axis, bit in (("pair", 1), ("dp", 1), ("dp", 2), ("dp", 4), ("dp", 8)):
+        v = v + flip(v, axis, bit)
+    return v
+
+
+def add16(a, b):
+    return (a.astype(F32) + b.astype(F32)).astype(BF16)
+
+
+def pick(index, cases):
+    return lax.select_n(index, *cases)
+
+
+def reduce_pieces(mine, theirs, z):
+    half = mine[0].shape[1] // 2
+    first, second = [None] * 4, [None] * 4
+    for t in (3, 2, 1, 0):
+        r = core_flip(theirs[t])
+        own_a, own_b, x_a, x_b, y_a, y_b, d_a, d_b = [
+            add16(mine[t][i, s], r[i, s]) for i in range(4) for s in (slice(0, half), slice(half, None))
+        ]
+        got_a = y_flip(d_a)
+        got_b = x_flip(d_b)
+        xb = x_flip(x_b)
+        ya = y_flip(y_a)
+        xa = x_flip(add16(x_a, got_a))
+        yb = y_flip(add16(y_b, got_b))
+        first[t] = (own_a.astype(F32) + xa.astype(F32) + ya.astype(F32)).astype(BF16)
+        second[t] = (own_b.astype(F32) + xb.astype(F32) + yb.astype(F32)).astype(BF16)
+    done = []
+    for part in (first, second):
+        moving = z_up(pick((z + 3) & 3, part))
+        moving = z_up(add16(pick((z + 2) & 3, part), moving))
+        moving = z_up(add16(pick((z + 1) & 3, part), moving))
+        done += [pick(z, part), moving]
+    return done
+
+
+def by_kind(granule, emit):
+    joint = granule < 24
+    wide = (granule >= 32) & (granule < 64)
+    pl.when(joint)(lambda: emit(3))
+    pl.when(wide)(lambda: emit(4))
+    pl.when(jnp.logical_not(joint | wide))(lambda: emit(1))
+
+
+def pack_kernel(info, flat, out0, out1):
+    for gi in range(3):
+
+        def emit(n, gi=gi):
+            m = GRAN // n
+            for layer, out in enumerate((out0, out1)):
+                for j in range(6):
+                    parts = [
+                        flat[pl.ds(12 * (GRAN * gi + p) + 2 * j + layer, m, stride=12 * n), :] for p in range(n)
+                    ]
+                    tile = parts[0] if n == 1 else jnp.concatenate(parts, 0)
+                    out[gi, :, 128 * j : 128 * (j + 1)] = tile.astype(BF16)
+
+        by_kind(3 * info[0] + gi, emit)
+
+
+def piece_places(info):
+    z, x, c, y = info[1], info[2], info[3], info[4]
+    places = []
+    for other in (0, 1):
+        for k in range(4):
+            cut = SPLIT[k]
+            for dx, dy, lo, hi in ((0, 0, 0, 3), (1, 0, 0, 3), (0, 1, 0, 3), (1, 1, 0, cut), (1, 1, cut, 3)):
+                dev = (
+                    8 * ((z + 4 - k) & 3)
+                    + 4 * jnp.bitwise_xor(x, dx)
+                    + 2 * jnp.bitwise_xor(c, other)
+                    + jnp.bitwise_xor(y, dy)
+                )
+                places.append((3 * dev + lo, hi - lo))
+    return places
+
+
+SPLIT = (1, 2, 1, 2)
+
+
+def fill(info, pieces, wbuf, sem):
+    copies = [
+        pltpu.make_async_copy(piece, wbuf.at[pl.ds(start, n)], sem.at[i])
+        for i, (piece, (start, n)) in enumerate(zip(pieces, piece_places(info)))
+    ]
+    for c in copies:
+        c.start()
+    return copies
+
+
+def split_w1(wbuf, w1):
+    def step(i, carry):
+        rows = wbuf[pl.ds(32 + 4 * i, 4)].astype(F32)
+        for j in range(4):
+            part = rows[:, 24 * j : 24 * (j + 1), :].reshape(GRAN, D).astype(BF16)
+            w1[j, pl.ds(pl.multiple_of(GRAN * i, GRAN), GRAN), :] = part
+        return carry
+
+    lax.fori_loop(0, 8, step, 0)
+
+
+def w_in(wbuf, j):
+    return wbuf[0:24, 32 * j : 32 * (j + 1), :].reshape(D, D)
+
+
+def w_out(wbuf):
+    return wbuf[24:32].reshape(D, D)
+
+
+def w_shrink(wbuf, j):
+    return wbuf[64 + 8 * j : 72 + 8 * j].reshape(D, D)
+
+
+def expander():
+    r, c = iota((32, 16), 0), iota((32, 16), 1)
+    return ((r < 24) & ((r & 1) == c)).astype(BF16)
+
+
+def head_mask():
+    r, lane = iota((32, D), 0), iota((32, D), 1)
+    return (r < 24) & ((r >> 1) == (lane >> 6))
+
+
+def spread(expand, mask, rows):
+    return jnp.where(mask, nn(expand, rows), 0.0).astype(BF16)
+
+
+def first_forward(
+    info, u_ref, vec, *refs
+):
+    pieces = refs[:40]
+    y_out, xh1_o, rs1_o, xh2_o, rs2_o, gp_o, e_o, h_o, att_o, u_o, q_o, pu_o, qk_o, p_o, wbuf, w1, sem = refs[40:]
+    copies = fill(info, pieces, wbuf, sem)
+    start = info[5]
+    u = u_ref[...]
+    r, t = iota((16, TOK), 0), iota((16, TOK), 1)
+    picker = (((r == 0) & (t == 0)) | ((r == 1) & (t == start))).astype(BF16)
+    cls = nn(picker, u)
+    cls16 = cls.astype(BF16)
+    expand, mask = expander(), head_mask()
+    r, t = iota((32, TOK), 0), iota((32, TOK), 1)
+    inside = (t >= start).astype(jnp.int32) == (r & 1)
+    real = r < 24
+    for c in copies:
+        c.wait()
+    split_w1(wbuf, w1)
+    q = (nn(cls16, w_in(wbuf, 0)) + vec[V_BQ : V_BQ + 1, :]).astype(BF16)
+    qk = nt(spread(expand, mask, q), w_in(wbuf, 1)).astype(BF16)
+    scores = jnp.where(inside, nt(qk, u) * HEAD_DIM**-0.5, masked_score)
+    raised = jnp.exp(scores - jnp.max(scores, axis=-1, keepdims=True))
+    portions = jnp.where(real, raised / jnp.sum(raised, axis=-1, keepdims=True), 0.0)
+    low = portions.astype(BF16)
+    pu = nn(low, u).astype(BF16)
+    weight = jnp.sum(low.astype(F32), axis=-1, keepdims=True)
+    heads = nn(pu, w_in(wbuf, 2)) + weight * vec[V_BV : V_BV + 1, :]
+    att = tn(expand, jnp.where(mask, heads, 0.0).astype(BF16)).astype(BF16)
+    xhat, rstd = norm_forward(cls + nn(att, w_out(wbuf)) + vec[V_BO : V_BO + 1, :])
+    xh1_o[...] = xhat
+    rs1_o[...] = jnp.broadcast_to(rstd, (16, 128))
+    h = xhat * vec[V_G1 : V_G1 + 1, :] + vec[V_C1 : V_C1 + 1, :]
+    h16 = h.astype(BF16)
+    f = vec[V_B2 : V_B2 + 1, :]
+    for j in range(4):
+        e, gp = gelu_both(nn(h16, w1[j]) + vec[V_B1 + j : V_B1 + j + 1, :])
+        e = e.astype(BF16)
+        e_o[j] = e
+        gp_o[j] = gp
+        f = f + nn(e, w_shrink(wbuf, j))
+    xhat, rstd = norm_forward(h + f)
+    xh2_o[...] = xhat
+    rs2_o[...] = jnp.broadcast_to(rstd, (16, 128))
+    y_out[...] = xhat * vec[V_G2 : V_G2 + 1, :] + vec[V_C2 : V_C2 + 1, :]
+    h_o[...] = h16
+    att_o[...] = att
+    u_o[...] = cls16
+    q_o[...] = q
+    pu_o[...] = pu
+    qk_o[...] = qk
+    p_o[...] = portions
+
+
+def first_backward(
+    info, u_ref, vec, cls_all, dz, xh1, rs1, xh2, rs2, gp_i, e_i, h_i, att_i, ucls, q_i, pu_i, qk_i, p_i, *refs
+):
+    pieces = refs[:40]
+    tg_out, pay_out, vg_out, loss_out, wbuf, w1, rows16, dcls, pay, sem = refs[40:]
+    copies = fill(info, pieces, wbuf, sem)
+    start = info[5]
+    u = u_ref[...]
+    keys = cls_all[...]
+    n_keys = keys.shape[0]
+    scale = 2.0 / math.sqrt(D)
+    r, c = iota((n_keys, n_keys), 0), iota((n_keys, n_keys), 1)
+    scores = jnp.where(r == c, masked_score, nt(keys, keys) * scale)
+    top = jnp.max(scores, axis=-1, keepdims=True)
+    raised = jnp.exp(scores - top)
+    total = jnp.sum(raised, axis=-1, keepdims=True)
+    partner = jnp.bitwise_xor(r, 2) == c
+    positive = jnp.sum(jnp.where(partner, scores, 0.0), axis=-1, keepdims=True)
+    terms = top + jnp.log(total) - positive
+    loss_out[...] = jnp.broadcast_to(colsum(terms) * (1.0 / n_keys), (8, 128))
+    pull = (raised / total - partner.astype(F32)).astype(BF16)
+    dcls[...] = (nn(pull, keys) + tn(pull, keys)) * scale
+    rows16[...] = jnp.zeros((16, D), F32)
+    rows16[0:1, :] = dz[0:1, :] + dcls[pl.ds(2 * info[0], 1), :]
+    rows16[1:2, :] = dz[pl.ds(start, 1), :] + dcls[pl.ds(2 * info[0] + 1, 1), :]
+    dy = rows16[...]
+    for copy in copies:
+        copy.wait()
+    split_w1(wbuf, w1)
+    vg_out[...] = jnp.zeros((16, D), F32)
+    xhat = xh2[...]
+    vg_out[V_G2 : V_G2 + 1, :] = colsum(dy * xhat)
+    vg_out[V_C2 : V_C2 + 1, :] = colsum(dy)
+    dr2 = norm_backward(dy, vec[V_G2 : V_G2 + 1, :], xhat, rs2[:, 0:1])
+    df = dr2.astype(BF16)
+    pay[R_DF : R_DF + 2, :] = df.astype(F32)[0:2, :]
+    vg_out[V_B2 : V_B2 + 1, :] = colsum(df.astype(F32))
+    dh = dr2
+    for j in range(4):
+        da = (gp_i[j] * nt(df, w_shrink(wbuf, j))).astype(BF16)
+        pay[R_E + 2 * j : R_E + 2 * j + 2, :] = e_i[j].astype(F32)[0:2, :]
+        pay[R_DA + 2 * j : R_DA + 2 * j + 2, :] = da.astype(F32)[0:2, :]
+        vg_out[V_B1 + j : V_B1 + j + 1, :] = colsum(da.astype(F32))
+        dh = dh + nt(da, w1[j])
+    xhat = xh1[...]
+    vg_out[V_G1 : V_G1 + 1, :] = colsum(dh * xhat)
+    vg_out[V_C1 : V_C1 + 1, :] = colsum(dh)
+    dr1 = norm_backward(dh, vec[V_G1 : V_G1 + 1, :], xhat, rs1[:, 0:1])
+    do = dr1.astype(BF16)
+    vg_out[V_BO : V_BO + 1, :] = colsum(do.astype(F32))
+    datt = nt(do, w_out(wbuf)).astype(BF16)
+    expand, mask = expander(), head_mask()
+    portions = p_i[...]
+    low = portions.astype(BF16)
+    each = spread(expand, mask, datt)
+    dvk = nt(each, w_in(wbuf, 2)).astype(BF16)
+    constant = jnp.sum(each.astype(F32) * vec[V_BV : V_BV + 1, :], axis=-1, keepdims=True)
+    dp = nt(dvk, u) + constant
+    ds = (portions * (dp - jnp.sum(dp * portions, axis=-1, keepdims=True))).astype(BF16)
+    dsu = nn(ds, u)
+    weight = jnp.sum(low.astype(F32), axis=-1, keepdims=True)
+    vg_out[V_BV : V_BV + 1, :] = colsum(each.astype(F32) * weight)
+    part = jnp.where(mask, nn(dsu.astype(BF16), w_in(wbuf, 1)) * HEAD_DIM**-0.5, 0.0).astype(BF16)
+    dq = tn(expand, part).astype(BF16)
+    vg_out[V_BQ : V_BQ + 1, :] = colsum(dq.astype(F32))
+    rows16[...] = dr1 + nt(dq, w_in(wbuf, 0))
+    du = tn(ds, qk_i[...]) * HEAD_DIM**-0.5 + tn(low, dvk)
+    is_cls = (iota((TOK, 1), 0) == 0) | (iota((TOK, 1), 0) == start)
+    tg_out[...] = du + jnp.where(is_cls, 0.0, dz[...])
+    tg_out[0:1, :] = tg_out[0:1, :] + rows16[0:1, :]
+    tg_out[pl.ds(start, 1), :] = tg_out[pl.ds(start, 1), :] + rows16[1:2, :]
+    for row, rows in ((R_H, h_i), (R_ATT, att_i), (R_U, ucls), (R_Q, q_i)):
+        pay[row : row + 2, :] = rows[...].astype(F32)[0:2, :]
+    for row, rows in ((R_DO, do), (R_DQ, dq), (R_DATT, datt)):
+        pay[row : row + 2, :] = rows.astype(F32)[0:2, :]
+    pay[R_WK : R_WK + 24, :] = dsu[0:24, :] * HEAD_DIM**-0.5
+    pay[R_PU : R_PU + 24, :] = pu_i[...].astype(F32)[0:24, :]
+    pay_out[...] = pay[...].astype(BF16)
+
+
+def second_block(info, u_ref, cot_ref, y_ref, vec, *refs):
+    pieces = refs[:40]
+    head_out, dz_out, vg_out = refs[40:43]
+    outs = refs[43:51]
+    (wbuf, w1, gbuf, zf, zb, qs, ks, vs, pm, att, xh1, hb, ht, gp, es, das, xh2, acc, stage, dqs, dks, dvs, sem, osem) = refs[51:]
+    copies = fill(info, pieces, wbuf, sem)
+    start = info[5]
+    zf[...] = u_ref[...].astype(F32)
+    zf[0:1, :] = y_ref[0:1, :]
+    zf[pl.ds(start, 1), :] = y_ref[1:2, :]
+    z16 = zf[...].astype(BF16)
+    zb[...] = z16
+    for c in copies:
+        c.wait()
+    split_w1(wbuf, w1)
+    qs[...] = (nn(z16, w_in(wbuf, 0)) + vec[V_BQ : V_BQ + 1, :]).astype(BF16)
+    ks[...] = nn(z16, w_in(wbuf, 1)).astype(BF16)
+    vs[...] = (nn(z16, w_in(wbuf, 2)) + vec[V_BV : V_BV + 1, :]).astype(BF16)
+    low_lane = iota((TOK, 128), 1) < HEAD_DIM
+    same = (iota((TOK, TOK), 0) >= start) == (iota((TOK, TOK), 1) >= start)
+
+    def lanes(p):
+        return pl.ds(pl.multiple_of(128 * p, 128), 128)
+
+    def attend(p, carry):
+        qp, kp, vp = qs[:, lanes(p)], ks[:, lanes(p)], vs[:, lanes(p)]
+        res = []
+        for hh in range(2):
+            qm = jnp.where(low_lane == (hh == 0), qp, jnp.zeros_like(qp))
+            s = jnp.where(same, nt(qm, kp) * HEAD_DIM**-0.5, masked_score)
+            raised = jnp.exp(s - jnp.max(s, axis=-1, keepdims=True))
+            portions = raised / jnp.sum(raised, axis=-1, keepdims=True)
+            pm[2 * p + hh] = portions
+            res.append(nn(portions.astype(BF16), vp))
+        att[:, lanes(p)] = jnp.where(low_lane, res[0], res[1]).astype(BF16)
+        return carry
+
+    lax.fori_loop(0, 6, attend, 0)
+    xhat, rstd1 = norm_forward(zf[...] + (nn(att[...], w_out(wbuf)) + vec[V_BO : V_BO + 1, :]))
+    xh1[...] = xhat
+    h = xhat * vec[V_G1 : V_G1 + 1, :] + vec[V_C1 : V_C1 + 1, :]
+    hb[...] = h.astype(BF16)
+    ht[...] = h.T.astype(BF16)
+    acc[...] = h + vec[V_B2 : V_B2 + 1, :]
+    for j in range(4):
+        e, slope = gelu_both(nn(hb[...], w1[j]) + vec[V_B1 + j : V_B1 + j + 1, :])
+        gp[j] = slope
+        e = e.astype(BF16)
+        es[j] = e
+        acc[...] += nn(e, w_shrink(wbuf, j))
+    xhat, rstd2 = norm_forward(acc[...])
+    xh2[...] = xhat
+    head_out[...] = (xhat * vec[V_G2 : V_G2 + 1, :] + vec[V_C2 : V_C2 + 1, :]).astype(BF16)
+
+    vg_out[...] = jnp.zeros((16, D), F32)
+    dy = cot_ref[...].astype(F32)
+    vg_out[V_G2 : V_G2 + 1, :] = colsum(dy * xh2[...])
+    vg_out[V_C2 : V_C2 + 1, :] = colsum(dy)
+    dr = norm_backward(dy, vec[V_G2 : V_G2 + 1, :], xh2[...], rstd2)
+    acc[...] = dr
+    df = dr.astype(BF16)
+    dqs[...] = df
+    vg_out[V_B2 : V_B2 + 1, :] = colsum(df.astype(F32))
+    for j in range(4):
+        df = dqs[...]
+        gbuf[64 + 8 * j : 72 + 8 * j] = tn(es[j], df).astype(BF16).reshape(8, GRAN, D)
+        da = (gp[j] * nt(df, w_shrink(wbuf, j))).astype(BF16)
+        das[j] = da
+        vg_out[V_B1 + j : V_B1 + j + 1, :] = colsum(da.astype(F32))
+        acc[...] += nt(da, w1[j])
+
+    def expand_grad(i, carry):
+        rows = ht[pl.ds(pl.multiple_of(192 * i, 192), 192), :]
+        for j in range(4):
+            stage[:, 24 * j : 24 * (j + 1), :] = nn(rows, das[j]).reshape(8, 24, D)
+        gbuf[pl.ds(32 + 8 * i, 8)] = stage[...].astype(BF16)
+        return carry
+
+    lax.fori_loop(0, 4, expand_grad, 0)
+    dh = acc[...]
+    vg_out[V_G1 : V_G1 + 1, :] = colsum(dh * xh1[...])
+    vg_out[V_C1 : V_C1 + 1, :] = colsum(dh)
+    dr = norm_backward(dh, vec[V_G1 : V_G1 + 1, :], xh1[...], rstd1)
+    acc[...] = dr
+    do = dr.astype(BF16)
+    vg_out[V_BO : V_BO + 1, :] = colsum(do.astype(F32))
+    gbuf[24:32] = tn(att[...], do).astype(BF16).reshape(8, GRAN, D)
+    att[...] = nt(do, w_out(wbuf)).astype(BF16)
+
+    def attend_back(p, carry):
+        qp, kp, vp, dp_ = qs[:, lanes(p)], ks[:, lanes(p)], vs[:, lanes(p)], att[:, lanes(p)]
+        dq, dk, dv = [], [], []
+        for hh in range(2):
+            portions = pm[2 * p + hh]
+            dam = jnp.where(low_lane == (hh == 0), dp_, jnp.zeros_like(dp_))
+            dp = nt(dam, vp)
+            dv.append(tn(portions.astype(BF16), dp_))
+            ds = (portions * (dp - jnp.sum(dp * portions, axis=-1, keepdims=True))).astype(BF16)
+            dq.append(nn(ds, kp))
+            dk.append(tn(ds, qp))
+        dqs[:, lanes(p)] = (jnp.where(low_lane, dq[0], dq[1]) * HEAD_DIM**-0.5).astype(BF16)
+        dks[:, lanes(p)] = (jnp.where(low_lane, dk[0], dk[1]) * HEAD_DIM**-0.5).astype(BF16)
+        dvs[:, lanes(p)] = jnp.where(low_lane, dv[0], dv[1]).astype(BF16)
+        return carry
+
+    lax.fori_loop(0, 6, attend_back, 0)
+    vg_out[V_BQ : V_BQ + 1, :] = colsum(dqs[...].astype(F32))
+    vg_out[V_BV : V_BV + 1, :] = colsum(dvs[...].astype(F32))
+    for j, part in enumerate((dqs, dks, dvs)):
+        gbuf[0:24, 32 * j : 32 * (j + 1), :] = tn(zb[...], part[...]).astype(BF16).reshape(24, 32, D)
+        acc[...] += nt(part[...], w_in(wbuf, j))
+    dz_out[...] = acc[...]
+    x, c, y = info[2], info[3], info[4]
+    sends = []
+    for t in (3, 2, 1, 0):
+        for other in (1, 0):
+            for rel in range(4):
+                dev = (
+                    8 * t
+                    + 4 * jnp.bitwise_xor(x, rel & 1)
+                    + 2 * jnp.bitwise_xor(c, other)
+                    + jnp.bitwise_xor(y, rel >> 1)
+                )
+                i = 4 * other + t
+                copy = pltpu.make_async_copy(gbuf.at[pl.ds(3 * dev, 3)], outs[i].at[rel], osem.at[4 * i + rel])
+                copy.start()
+                sends.append(copy)
+    for copy in sends:
+        copy.wait()
+
+
+def owner_grad(info, *refs):
+    pieces = refs[:40]
+    out, pbuf, pf, sem = refs[40:]
+    copies = []
+    n = 0
+    for other in range(2):
+        for k in range(4):
+            for slot, lo, hi in ((0, 0, PAY), (1, 0, PAY), (2, 0, PAY), (3, 0, PAY_A), (3, PAY_A, PAY)):
+                dst = pbuf.at[16 * other + 4 * k + slot, pl.ds(lo, hi - lo)]
+                copies.append(pltpu.make_async_copy(pieces[n], dst, sem.at[n]))
+                n += 1
+    for c in copies:
+        c.start()
+    for c in copies:
+        c.wait()
+
+    def widen(i, carry):
+        for j in range(6):
+            pf[j, pl.ds(pl.multiple_of(PAY * i, PAY), PAY), :] = pbuf[i, :, 128 * j : 128 * (j + 1)].astype(F32)
+        return carry
+
+    lax.fori_loop(0, 32, widen, 0)
+
+    def rows(first):
+        return jnp.concatenate(
+            [
+                jnp.concatenate(
+                    [pf[j, pl.ds(first + s, 32, stride=PAY), :] for j in range(6)], axis=1
+                )
+                for s in range(2)
+            ],
+            axis=0,
+        ).astype(BF16)
+
+    def chosen(count, offset, source):
+        one_hot = (iota((count, D), 1) == iota((count, D), 0) + offset).astype(BF16)
+        return nt(one_hot, source).astype(BF16)
+
+    def put(gi, n, p, value):
+        m = GRAN // n
+        for j in range(6):
+            out[pl.ds(6 * (GRAN * gi + p) + j, m, stride=6 * n), :] = value[:, 128 * j : 128 * (j + 1)]
+
+    for gi in range(3):
+        g = 3 * info[0] + gi
+
+        @pl.when(g < 24)
+        def _(gi=gi, g=g):
+            off = 32 * g
+            put(gi, 3, 0, nn(chosen(32, off, rows(R_U)), rows(R_DQ)))
+            lane = iota((64, D), 1) >> 6
+            for p, left, right in ((1, R_WK, R_Q), (2, R_PU, R_DATT)):
+                base = rows(right)
+                total = jnp.zeros((32, D), F32)
+                for h in range(HEADS):
+                    masked = jnp.where(lane == h, base, jnp.zeros_like(base))
+                    total = total + nn(chosen(32, off, rows(left + 2 * h)), masked)
+                put(gi, 3, p, total)
+
+        @pl.when((g >= 24) & (g < 32))
+        def _(gi=gi, g=g):
+            put(gi, 1, 0, nn(chosen(GRAN, GRAN * (g - 24), rows(R_ATT)), rows(R_DO)))
+
+        @pl.when((g >= 32) & (g < 64))
+        def _(gi=gi, g=g):
+            left = chosen(24, 24 * (g - 32), rows(R_H))
+            for p in range(4):
+                put(gi, 4, p, nn(left, rows(R_DA + 2 * p)))
+
+        @pl.when(g >= 64)
+        def _(gi=gi, g=g):
+            part = (g - 64) >> 3
+            put(gi, 1, 0, nn(chosen(GRAN, GRAN * ((g - 64) & 7), rows(R_E + 2 * part)), rows(R_DF)))
+
+
+def join_grads(info, g0, a1, a2, b1, b2, out, square, buf):
+    g = g0[...]
+    out[pl.ds(0, 1728, stride=2), :] = g
+    buf[0:144, :] = a1[...].astype(F32) + a2[...].astype(F32)
+    buf[144:288, :] = b1[...].astype(F32) + b2[...].astype(F32)
+    total = buf[...]
+    sq = jnp.sum((g * g).reshape(216, 8, 128), axis=0)
+    for j in range(6):
+        v = total[:, 128 * j : 128 * (j + 1)]
+        sq = sq + jnp.sum((v * v).reshape(36, 8, 128), axis=0)
+    square[...] = sq
+    for gi in range(3):
+
+        def emit(n, gi=gi):
+            m = GRAN // n
+            for p in range(n):
+                for j in range(6):
+                    out[pl.ds(12 * (GRAN * gi + p) + 2 * j + 1, m, stride=12 * n), :] = buf[
+                        GRAN * gi + m * p : GRAN * gi + m * (p + 1), 128 * j : 128 * (j + 1)
+                    ]
+
+        by_kind(3 * info[0] + gi, emit)
+
+
+def adamw_kernel(coef, w, m, v, g, w_out_, m_out, v_out):
+    new = adamw_update(w[...], m[...], v[...], g[...] * coef[0], 0.1, weight_decay)
+    w_out_[...], m_out[...], v_out[...] = new
+
+
+def adamw_update(weight, moment_one, moment_two, gradient, step_rate, decay_rate):
+    first_new = beta_one * moment_one + (1.0 - beta_one) * gradient
+    second_new = beta_two * moment_two + (1.0 - beta_two) * gradient * gradient
+    first_hat = first_new / (1.0 - beta_one**STEP)
+    second_hat = second_new / (1.0 - beta_two**STEP)
+    weight_new = weight - step_rate * (first_hat / (jnp.sqrt(second_hat) + adam_epsilon) + decay_rate * weight)
+    return (weight_new, first_new, second_new)
+
+
+SMEM = pl.BlockSpec(memory_space=pltpu.SMEM)
+VMEM = pl.BlockSpec(memory_space=pltpu.VMEM)
+ANY = pl.BlockSpec(memory_space=pl.ANY)
+
+
+def struct(*shape, dtype=F32):
+    return jax.ShapeDtypeStruct(shape, dtype)
+
+
+def call(kernel, name, ins, in_specs, outs, out_specs, scratch=(), flops=0, moved=0):
+    return pl.pallas_call(
+        kernel,
+        out_shape=outs,
+        in_specs=in_specs,
+        out_specs=out_specs,
+        scratch_shapes=list(scratch),
+        name=name,
+        compiler_params=pltpu.CompilerParams(vmem_limit_bytes=VMEM_BYTES),
+        cost_estimate=pl.CostEstimate(flops=flops, bytes_accessed=moved, transcendentals=0),
+    )(*ins)
+
+
+def flat_view(a):
+    return a.reshape(2, -1, 128).transpose(1, 0, 2).reshape(-1, 128)
+
+
+def flat_back(a):
+    return a.reshape(-1, 2, 128).transpose(1, 0, 2).reshape(2, -1)
+
+
+def body(tokens, cotangent, lengths, mats, mats_m, mats_v, vecs, vecs_m, vecs_v):
+    dp, pair = lax.axis_index("dp"), lax.axis_index("pair")
+    device = 2 * dp + pair
+    z = dp >> 2
+    info = jnp.stack(
+        [device, z, (dp >> 1) & 1, dp & 1, pair, lengths[0, 0, 0], jnp.int32(0), jnp.int32(0)]
+    ).astype(jnp.int32)
+    u = tokens[0]
+    cot = cotangent[0]
+    shard = struct(3, GRAN, D, dtype=BF16)
+    flat = flat_view(mats)
+    own0, own1 = call(pack_kernel, "pack", (info, flat), [SMEM, VMEM], (shard, shard), (VMEM, VMEM))
+    pieces0 = gather_pieces(own0, SPLIT)
+    every_vec = doubled(vecs.astype(BF16).reshape(1, -1), dp, pair)
+    every_vec = every_vec.reshape(32, 2, -1).transpose(1, 0, 2).reshape(2, 12, D).astype(F32)
+    every_vec = jnp.pad(every_vec, ((0, 0), (0, 4), (0, 0)))
+    vec0, vec1 = every_vec[0], every_vec[1]
+    row = struct(16, D)
+    row16 = struct(16, D, dtype=BF16)
+    saved_shapes = (
+        row, struct(16, 128), row, struct(16, 128), struct(4, 16, D), struct(4, 16, D, dtype=BF16),
+        row16, row16, row16, row16, struct(32, D, dtype=BF16), struct(32, D, dtype=BF16), struct(32, TOK),
+    )
+    weights = [
+        pltpu.VMEM((GRANS, GRAN, D), BF16),
+        pltpu.VMEM((4, D, D), BF16),
+    ]
+    y_cls, *saved = call(
+        first_forward,
+        "first_forward",
+        (info, u, vec0, *pieces0),
+        [SMEM, VMEM, VMEM] + [ANY] * 40,
+        (row, *saved_shapes),
+        (VMEM,) * 14,
+        weights + [pltpu.SemaphoreType.DMA((40,))],
+        flops=2 * 32 * PL,
+        moved=2 * PL,
+    )
+    every_cls = doubled(y_cls[0:2].astype(BF16), dp, pair)
+    pieces1 = gather_pieces(own1, SPLIT)
+    part = struct(4, 3, GRAN, D, dtype=BF16)
+    mid16 = pltpu.VMEM((TOK, D), BF16)
+    mid = pltpu.VMEM((TOK, D), F32)
+    head_out, dz, vg1, *terms = call(
+        second_block,
+        "second_block",
+        (info, u, cot, y_cls, vec1, *pieces1),
+        [SMEM, VMEM, VMEM, VMEM, VMEM] + [ANY] * 40,
+        (struct(TOK, D, dtype=BF16), struct(TOK, D), row) + (part,) * 8,
+        (VMEM, VMEM, VMEM) + (ANY,) * 8,
+        weights
+        + [
+            pltpu.VMEM((GRANS, GRAN, D), BF16),
+            mid, mid16, mid16, mid16, mid16,
+            pltpu.VMEM((HEADS, TOK, TOK), F32),
+            mid16, mid, mid16,
+            pltpu.VMEM((D, TOK), BF16),
+            pltpu.VMEM((4, TOK, D), F32),
+            pltpu.VMEM((4, TOK, D), BF16),
+            pltpu.VMEM((4, TOK, D), BF16),
+            mid, mid,
+            pltpu.VMEM((8, GRAN, D), F32),
+            mid16, mid16, mid16,
+            pltpu.SemaphoreType.DMA((40,)),
+            pltpu.SemaphoreType.DMA((32,)),
+        ],
+        flops=6 * TOK * PL,
+        moved=4 * PL,
+    )
+    terms = [t.reshape(4, 288, D) for t in terms]
+    a1, a2, b1, b2 = reduce_pieces(terms[:4], terms[4:], z)
+    token_grad, payload, vg0, loss = call(
+        first_backward,
+        "first_backward",
+        (info, u, vec0, every_cls, dz, *saved, *pieces0),
+        [SMEM] + [VMEM] * 17 + [ANY] * 40,
+        (struct(TOK, D), struct(PAY, D, dtype=BF16), row, struct(8, 128)),
+        (VMEM,) * 4,
+        weights
+        + [
+            pltpu.VMEM((16, D), F32),
+            pltpu.VMEM((64, D), F32),
+            pltpu.VMEM((PAY, D), F32),
+            pltpu.SemaphoreType.DMA((40,)),
+        ],
+        flops=2 * 32 * PL,
+        moved=2 * PL,
+    )
+    flat0 = call(
+        owner_grad,
+        "owner_grad",
+        (info, *gather_pieces(payload, (PAY_A,) * 4)),
+        [SMEM] + [ANY] * 40,
+        struct(1728, 128),
+        VMEM,
+        [
+            pltpu.VMEM((32, PAY, D), BF16),
+            pltpu.VMEM((6, 32 * PAY, 128), F32),
+            pltpu.SemaphoreType.DMA((40,)),
+        ],
+        flops=2 * 768 * 768 * 768,
+        moved=2 * 32 * PAY * D,
+    )
+    vec_sum = summed(jnp.concatenate([vg0[:12], vg1[:12]], 0)).reshape(2, QL)
+    grad_vecs = lax.dynamic_slice(vec_sum, (0, device * vecs.shape[1]), vecs.shape)
+    grads, square = call(
+        join_grads,
+        "join_grads",
+        (info, flat0, a1, a2, b1, b2),
+        [SMEM] + [VMEM] * 5,
+        (struct(3456, 128), struct(8, 128)),
+        (VMEM, VMEM),
+        [pltpu.VMEM((288, D), F32)],
+    )
+    square_sum = jnp.sum(square) + jnp.sum(grad_vecs * grad_vecs)
+    total_sq = summed(jnp.broadcast_to(square_sum, (8, 128)))[0, 0]
+    grad_norm = jnp.sqrt(total_sq)
+    clip_factor = jnp.minimum(1.0, math.sqrt(2 * (PL + QL)) / (grad_norm + 1e-06))
+    block = pl.BlockSpec((432, 128), lambda i: (i, 0))
+    new = pl.pallas_call(
+        adamw_kernel,
+        grid=(8,),
+        in_specs=[SMEM] + [block] * 4,
+        out_specs=(block,) * 3,
+        out_shape=(struct(3456, 128),) * 3,
+        name="adamw",
+    )(clip_factor.reshape(1), flat, flat_view(mats_m), flat_view(mats_v), grads)
+    new_mats, new_mats_m, new_mats_v = [flat_back(a) for a in new]
+    new_vecs, new_vecs_m, new_vecs_v = adamw_update(vecs, vecs_m, vecs_v, grad_vecs * clip_factor, 0.5, 0.0)
+    return (
+        head_out[None],
+        token_grad[None],
+        loss[0, 0],
+        grad_norm,
+        new_mats,
+        new_mats_m,
+        new_mats_v,
+        new_vecs,
+        new_vecs_m,
+        new_vecs_v,
+    )
 
 
 def matmul(left_side, right_side):
@@ -261,18 +1062,7 @@
     return (grads_low, logsum - positive)
 
 
-def adamw_update(weight, moment_one, moment_two, gradient, step_rate, decay_rate):
-    first_new = beta_one * moment_one + (1.0 - beta_one) * gradient
-    second_new = beta_two * moment_two + (1.0 - beta_two) * gradient * gradient
-    first_hat = first_new / (1.0 - beta_one**STEP)
-    second_hat = second_new / (1.0 - beta_two**STEP)
-    weight_new = weight - step_rate * (
-        first_hat / (jnp.sqrt(second_hat) + adam_epsilon) + decay_rate * weight
-    )
-    return (weight_new, first_new, second_new)
-
-
-def body(tokens, cotangent, lengths, mats, mats_m, mats_v, vecs, vecs_m, vecs_v):
+def general_body(tokens, cotangent, lengths, mats, mats_m, mats_v, vecs, vecs_m, vecs_v):
     full_mats, full_vecs = (
         lax.all_gather(mats.astype(jnp.bfloat16), ("dp", "pair"), axis=1, tiled=True),
         lax.all_gather(vecs.astype(jnp.bfloat16), ("dp", "pair"), axis=1, tiled=True),
@@ -284,7 +1074,8 @@
     span_lengths = lengths[0, 0]
     span_count = span_lengths.shape[0]
     positions = jnp.arange(row_count, dtype=jnp.int32)
-    starts = jnp.cumsum(span_lengths) - span_lengths
+    order = jnp.arange(span_count)
+    starts = jnp.sum(jnp.where(order[None, :] < order[:, None], span_lengths[None, :], 0), axis=1)
     span_of = jnp.sum((positions[:, None] >= starts[None, :]).astype(jnp.int32), axis=1)
     same_span = span_of[:, None] == span_of[None, :]
     heads_mark = positions[None, :] == starts[:, None]
@@ -399,31 +1190,13 @@
 
 
 def solution(mesh):
+    flat = P(None, ("dp", "pair"))
+    rows = P("pair", "dp", None)
+    here = dict(mesh.shape) == {"dp": 16, "pair": 2}
     return jax.shard_map(
-        body,
+        body if here else general_body,
         mesh=mesh,
-        in_specs=(
-            P("pair", "dp", None),
-            P("pair", "dp", None),
-            P("pair", "dp", None),
-            P(None, ("dp", "pair")),
-            P(None, ("dp", "pair")),
-            P(None, ("dp", "pair")),
-            P(None, ("dp", "pair")),
-            P(None, ("dp", "pair")),
-            P(None, ("dp", "pair")),
-        ),
-        out_specs=(
-            P("pair", "dp", None),
-            P("pair", "dp", None),
-            P(),
-            P(),
-            P(None, ("dp", "pair")),
-            P(None, ("dp", "pair")),
-            P(None, ("dp", "pair")),
-            P(None, ("dp", "pair")),
-            P(None, ("dp", "pair")),
-            P(None, ("dp", "pair")),
-        ),
+        in_specs=(rows, rows, rows) + (flat,) * 6,
+        out_specs=(rows, rows, P(), P()) + (flat,) * 6,
         check_vma=False,
     )

time: 1600 us -> 513 us (0.32)
  local copies, waits for them, and re-layouts: 478 us -> 22.9 us
  other arithmetic: 335 us -> 28.4 us
  blocking collectives: 182 us -> 0 us
  waiting for transfers between devices: 351 us -> 247 us
  matrix products: 90.9 us -> 0 us
  Pallas kernels: 0 us -> 90.8 us
  starting transfers between devices: 130 us -> 112 us
  between operations: 22 us -> 5.78 us
    ppermute x0 -> x171, waiting for transfers between devices: none -> 247 us  [the longest x156 202 us: flip(): lax.ppermute(v, axis, [(i, i ^ bit) for i in range(lax.axis_size(axis))])]
    all_to_all x4 -> x0, waiting for transfers between devices: 230 us -> none  [the longest x1 200 us: body(): lax.all_to_all(early_mats.reshape(doc_groups, -1).astype(jnp.bfloat16), '...]
    slice x10 -> x27, local copies, waits for them, and re-layouts: 219 us -> 5.98 us  [the longest x24 3.53 us: gather_pieces(): out += [slot, over_x, over_y, y_flip(over_x[:cut]), x_flip(over_y[cut:])]]
    convert_element_type x10 -> x14, other arithmetic: 176 us -> 10.8 us  [the longest x12 9.17 us: add16(): return (a.astype(F32) + b.astype(F32)).astype(BF16)]
    all_gather x2 -> x0, blocking collectives: 137 us -> none  [the longest x1 71.6 us: body(): lax.all_gather(vecs.astype(jnp.bfloat16), ('dp', 'pair'), axis=1, tiled=T...]
    all_to_all x4 -> x0, starting transfers between devices: 130 us -> none  [the longest x1 59.7 us: body(): lax.all_to_all(early_mats.reshape(doc_groups, -1).astype(jnp.bfloat16), '...]
    unnamed x335 -> x258, local copies, waits for them, and re-layouts: 121 us -> 6.82 us
    ppermute x0 -> x171, starting transfers between devices: none -> 112 us  [the longest x156 105 us: flip(): lax.ppermute(v, axis, [(i, i ^ bit) for i in range(lax.axis_size(axis))])]
  transfers between devices with their start and end apart: 7 -> 171, of which waited for: 6 -> 75; matrix products, arithmetic and copies ran while one was open for 30% -> 8% of each run, Pallas kernels for 0% -> 16%
where the time goes in v1:
time: 513 us; the launch traced here: 507 us
  waiting for transfers between devices  247 us (48%)
  starting transfers between devices  112 us (22%)
  Pallas kernels  90.8 us (18%)
  other arithmetic  28.4 us (6%)
  local copies, waits for them, and re-layouts  22.9 us (4%)
  between operations  5.78 us (1%)
    ppermute x156, waiting for transfers between devices, flip(): lax.ppermute(v, axis, [(i, i ^ bit) for i in range(lax.axis_size(axis))])  202 us
    ppermute x156, starting transfers between devices, flip(): lax.ppermute(v, axis, [(i, i ^ bit) for i in range(lax.axis_size(axis))])  105 us
    pallas_call x6, Pallas kernels, call(): pl.pallas_call(kernel, out_shape=outs, in_specs=in_specs, out_specs=out_s...  82.6 us
    ppermute x15, waiting for transfers between devices, z_up(): return lax.ppermute(v, 'dp', [(i, (i + 4) % n) for i in range(n)])  44.9 us
  transfers between devices with their start and end apart: 171, of which 75 were waited for; matrix products, arithmetic and copies ran while one was open for 8% of the time, Pallas kernels for 16%

profile of v1, /device:TPU:0, one launch (start us, length us, event | category | flops | bytes accessed | tf_op | source)
XLA Modules:
  0.0 507.0 jit_solution(14913849830782061551)
XLA Ops:
  13.7 6.5 %collective-permute-done.2 = bf16[4,576]{1,0:T(4,128)(2,1)S(1)} collective-permute-done((bf16[4,576]{1,0:T(4,128)(2,1)S(1)}, bf16[4,576]{1,0:T(4,128)(2,1)S(1)}, u32[]{:S(2)}, u32[]{:S(2)}) %collective-permute-start.2) | collective-permute-done | bytes 4640 | tf_op jit(solution)/shard_map/ppermute | solution.py:99
  34.4 5.0 collective-permute-done.44.refs_1_
  52.7 8.8 %collective-permute-done.47.refs_4_ = bf16[2,96,768]{2,1,0:T(8,128)(2,1)S(1)} collective-permute-done((bf16[2,96,768]{2,1,0:T(8,128)(2,1)S(1)}, bf16[2,96,768]{2,1,0:T(8,128)(2,1)S(1)}, u32[]{:S(2)}, u32[]{:S(2)}) %collective-permute-start.47) | collective-permute-done | bytes 294944 | tf_op jit(solution)/shard_map/ppermute | solution.py:99
  67.9 6.9 %collective-permute-done.49.refs_6_ = bf16[3,96,768]{2,1,0:T(8,128)(2,1)S(1)} collective-permute-done((bf16[3,96,768]{2,1,0:T(8,128)(2,1)S(1)}, bf16[3,96,768]{2,1,0:T(8,128)(2,1)S(1)}, u32[]{:S(2)}, u32[]{:S(2)}) %collective-permute-start.49) | collective-permute-done | bytes 442400 | tf_op jit(solution)/shard_map/ppermute | solution.py:99
  93.1 12.5 %collective-permute-done.12.refs_8_ = bf16[2,96,768]{2,1,0:T(8,128)(2,1)S(1)} collective-permute-done((bf16[2,96,768]{2,1,0:T(8,128)(2,1)S(1)}, bf16[2,96,768]{2,1,0:T(8,128)(2,1)S(1)}, u32[]{:S(2)}, u32[]{:S(2)}) %collective-permute-start.12) | collective-permute-done | bytes 294944 | tf_op jit(solution)/shard_map/ppermute | solution.py:99
  105.6 4.6 collective-permute-done.51.refs_8_
  114.6 8.3 %collective-permute-done.54.refs_11_ = bf16[3,96,768]{2,1,0:T(8,128)(2,1)S(1)} collective-permute-done((bf16[3,96,768]{2,1,0:T(8,128)(2,1)S(1)}, bf16[3,96,768]{2,1,0:T(8,128)(2,1)S(1)}, u32[]{:S(2)}, u32[]{:S(2)}) %collective-permute-start.54) | collective-permute-done | bytes 442400 | tf_op jit(solution)/shard_map/ppermute | solution.py:99
  139.8 13.7 %collective-permute-done.57.refs_14_ = bf16[2,96,768]{2,1,0:T(8,128)(2,1)S(1)} collective-permute-done((bf16[2,96,768]{2,1,0:T(8,128)(2,1)S(1)}, bf16[2,96,768]{2,1,0:T(8,128)(2,1)S(1)}, u32[]{:S(2)}, u32[]{:S(2)}) %collective-permute-start.57) | collective-permute-done | bytes 294944 | tf_op jit(solution)/shard_map/ppermute | solution.py:99
  161.9 5.6 %collective-permute-done.59.refs_16_ = bf16[3,96,768]{2,1,0:T(8,128)(2,1)} collective-permute-done((bf16[3,96,768]{2,1,0:T(8,128)(2,1)}, bf16[3,96,768]{2,1,0:T(8,128)(2,1)}, u32[]{:S(2)}, u32[]{:S(2)}) %collective-permute-start.59) | collective-permute-done | bytes 442400 | tf_op jit(solution)/shard_map/ppermute | solution.py:99
  184.2 11.4 %first_forward.1 = (f32[16,768]{1,0:T(8,128)}, f32[16,768]{1,0:T(8,128)}, f32[16,128]{1,0:T(8,128)}, f32[16,768]{1,0:T(8,128)}, f32[16,128]{1,0:T(8,128)}, /*ind...) custom-call(s32[8]{0:T(128)} %stack.23.info, ...), custom_call_target="tpu_custom_call" | custom-call | flops 452984832 | bytes 14155776 | tf_op jit(solution)/shard_map/first_forward/pallas_call | solution.py:663
  214.3 40.4 %second_block.1 = (bf16[256,768]{1,0:T(8,128)(2,1)}, f32[256,768]{1,0:T(8,128)}, f32[16,768]{1,0:T(8,128)}, bf16[4,3,96,768]{3,2,1,0:T(8,128)(2,1)}, bf16[4,3,96...) custom-call(s32[8]{0:T(128)} %stack.23.info, ...), custom_call_target="tpu_custom_call" | custom-call | flops 10871635968 | bytes 28311552 | tf_op jit(solution)/shard_map/second_block/pallas_call | solution.py:663
  255.6 13.2 %first_backward.1 = (f32[256,768]{1,0:T(8,128)}, bf16[80,768]{1,0:T(8,128)(2,1)}, f32[16,768]{1,0:T(8,128)}, f32[8,128]{1,0:T(8,128)}) custom-call(s32[8]{0:T(128)} %stack.23.info, bf16[256,768]{1,0:T(8,128)(2,1)} %bitcast.202, f32[16,768]{1,0:T(8,128)} %get-tuple-element.120.vec, bf16[64,768]{1,0:T(8,128)(2,1)} %maximum_select_fusion.cls_all, ...), custom_call_target="tpu_custom_call" | custom-call | flops 452984832 | bytes 14155776 | tf_op jit(solution)/shard_map/first_backward/pallas_call | solution.py:663
  278.2 4.8 collective-permute-done.92.refs_5_
  304.6 4.5 collective-permute-done.164
  319.5 6.2 %collective-permute-done.102.refs_15_ = bf16[80,768]{1,0:T(8,128)(2,1)S(1)} collective-permute-done((bf16[80,768]{1,0:T(8,128)(2,1)S(1)}, bf16[80,768]{1,0:T(8,128)(2,1)S(1)}, u32[]{:S(2)}, u32[]{:S(2)}) %collective-permute-start.102) | collective-permute-done | bytes 122912 | tf_op jit(solution)/shard_map/ppermute | solution.py:116
  344.8 5.0 collective-permute-done.165
  360.5 4.3 collective-permute-done.150
  410.7 11.7 %owner_grad.1.g0 = f32[1728,128]{1,0:T(8,128)} custom-call(s32[8]{0:T(128)} %stack.23.info, bf16[80,768]{1,0:T(8,128)(2,1)} %get-tuple-element.66.refs_0_, bf16[80,768]{1,0:T(8,128)(2,1)} %copy-done.37, bf16[80,768]{1,0:T(8,128)(2,1)} %copy-done.42, bf16[48,768]{1,0:T(8,128)(2,1)} %copy-done.78, bf16[32,768]{1,0:T(8,128)(2,1)} %copy-done.85, ...), custom_call_target="tpu_custom_call" | custom-call | flops 905969664 | bytes 3932160 | tf_op jit(solution)/shard_map/owner_grad/pallas_call | solution.py:663
  431.7 4.7 collective-permute-done.148
  436.4 4.3 collective-permute-done.157
  446.2 8.0 %collective-permute-done.158 = bf16[144,768]{1,0:T(8,128)(2,1)S(1)} collective-permute-done((bf16[144,768]{1,0:T(8,128)(2,1)S(1)}, bf16[144,768]{1,0:T(8,128)(2,1)S(1)}, u32[]{:S(2)}, u32[]{:S(2)}) %collective-permute-start.158) | collective-permute-done | bytes 221216 | tf_op jit(solution)/shard_map/ppermute | solution.py:116
  454.4 4.5 collective-permute-done.144
  459.2 4.4 collective-permute-done.159
  497.4 8.2 %adamw.1 = (f32[3456,128]{1,0:T(8,128)}, f32[3456,128]{1,0:T(8,128)}, f32[3456,128]{1,0:T(8,128)}) custom-call(f32[1]{0:T(128)} %bitcast.58.coef, f32[3456,128]{1,0:T(8,128)} %bitcast.181, f32[3456,128]{1,0:T(8,128)} %bitcast.182, f32[3456,128]{1,0:T(8,128)} %bitcast.183, f32[3456,128]{1,0:T(8,128)} %get-tuple-element.78.g), custom_call_target="tpu_custom_call" | custom-call | tf_op jit(solution)/shard_map/adamw/pallas_call | solution.py:802
  (668 shorter events, 293.6 us)
Async XLA Ops:
  8.3 22.0 %collective-permute-start.5 = (bf16[3,96,768]{2,1,0:T(8,128)(2,1)}, bf16[3,96,768]{2,1,0:T(8,128)(2,1)S(1)}, u32[]{:S(2)}, u32[]{:S(2)}) collective-permute-start(bf16[3,96,768]{2,1,0:T(8,128)(2,1)} %get-tuple-element.46.refs_0_), channel_id=1, source_target_pairs={{0,4},{2,6},{4,0},{6,2},{8,12},{10,14},{12,8},{14,10},{16,20},{18,... | collective-permute-start | bytes 1327112 | tf_op jit(solution)/shard_map/ppermute | solution.py:99
  9.7 21.0 %collective-permute-start.6 = (bf16[3,96,768]{2,1,0:T(8,128)(2,1)}, bf16[3,96,768]{2,1,0:T(8,128)(2,1)S(1)}, u32[]{:S(2)}, u32[]{:S(2)}) collective-permute-start(bf16[3,96,768]{2,1,0:T(8,128)(2,1)} %get-tuple-element.46.refs_0_), channel_id=1, source_target_pairs={{0,1},{1,0},{2,3},{3,2},{4,5},{5,4},{6,7},{7,6},{8,9},{9,8},{10,11... | collective-permute-start | bytes 1327112 | tf_op jit(solution)/shard_map/ppermute | solution.py:99
  10.2 22.5 %collective-permute-start.9 = (bf16[3,96,768]{2,1,0:T(8,128)(2,1)}, bf16[3,96,768]{2,1,0:T(8,128)(2,1)S(1)}, u32[]{:S(2)}, u32[]{:S(2)}) collective-permute-start(bf16[3,96,768]{2,1,0:T(8,128)(2,1)} %get-tuple-element.46.refs_0_), channel_id=1, source_target_pairs={{0,8},{2,10},{4,12},{6,14},{8,16},{10,18},{12,20},{14,22},{16,24},... | collective-permute-start | bytes 1327112 | tf_op jit(solution)/shard_map/ppermute | solution.py:116
  41.7 20.4 %collective-permute-start.10 = (bf16[3,96,768]{2,1,0:T(8,128)(2,1)S(1)}, bf16[3,96,768]{2,1,0:T(8,128)(2,1)S(1)}, u32[]{:S(2)}, u32[]{:S(2)}) collective-permute-start(bf16[3,96,768]{2,1,0:T(8,128)(2,1)S(1)} %collective-permute-done.9.refs_5_), channel_id=1, source_target_pairs={{0,4},{2,6},{4,0},{6,2},{8,12},{10,14},{12,8},{14,10},{16,20},{18,... | collective-permute-start | bytes 1327112 | tf_op jit(solution)/shard_map/ppermute | solution.py:99
  81.7 28.6 %collective-permute-start.15 = (bf16[3,96,768]{2,1,0:T(8,128)(2,1)S(1)}, bf16[3,96,768]{2,1,0:T(8,128)(2,1)S(1)}, u32[]{:S(2)}, u32[]{:S(2)}) collective-permute-start(bf16[3,96,768]{2,1,0:T(8,128)(2,1)S(1)} %collective-permute-done.14.refs_10_), channel_id=1, source_target_pairs={{0,4},{2,6},{4,0},{6,2},{8,12},{10,14},{12,8},{14,10},{16,20},{18,... | collective-permute-start | bytes 1327112 | tf_op jit(solution)/shard_map/ppermute | solution.py:99
  86.2 24.6 %collective-permute-start.16 = (bf16[3,96,768]{2,1,0:T(8,128)(2,1)S(1)}, bf16[3,96,768]{2,1,0:T(8,128)(2,1)S(1)}, u32[]{:S(2)}, u32[]{:S(2)}) collective-permute-start(bf16[3,96,768]{2,1,0:T(8,128)(2,1)S(1)} %collective-permute-done.14.refs_10_), channel_id=1, source_target_pairs={{0,1},{1,0},{2,3},{3,2},{4,5},{5,4},{6,7},{7,6},{8,9},{9,8},{10,11... | collective-permute-start | bytes 1327112 | tf_op jit(solution)/shard_map/ppermute | solution.py:99
  90.2 20.0 %collective-permute-start.51 = (bf16[2,96,768]{2,1,0:T(8,128)(2,1)S(1)}, bf16[2,96,768]{2,1,0:T(8,128)(2,1)S(1)}, u32[]{:S(2)}, u32[]{:S(2)}) collective-permute-start(bf16[2,96,768]{2,1,0:T(8,128)(2,1)S(1)} %slice.397), channel_id=1, source_target_pairs={{0,1},{1,0},{2,3},{3,2},{4,5},{5,4},{6,7},{7,6},{8,9},{9,8},{10,11... | collective-permute-start | bytes 884744 | tf_op jit(solution)/shard_map/ppermute | solution.py:99
  129.9 24.1 %collective-permute-start.20 = (bf16[3,96,768]{2,1,0:T(8,128)(2,1)S(1)}, bf16[3,96,768]{2,1,0:T(8,128)(2,1)S(1)}, u32[]{:S(2)}, u32[]{:S(2)}) collective-permute-start(bf16[3,96,768]{2,1,0:T(8,128)(2,1)S(1)} %collective-permute-done.19.refs_15_), channel_id=1, source_target_pairs={{0,4},{2,6},{4,0},{6,2},{8,12},{10,14},{12,8},{14,10},{16,20},{18,... | collective-permute-start | bytes 1327112 | tf_op jit(solution)/shard_map/ppermute | solution.py:99
  132.9 20.6 %collective-permute-start.57 = (bf16[2,96,768]{2,1,0:T(8,128)(2,1)S(1)}, bf16[2,96,768]{2,1,0:T(8,128)(2,1)S(1)}, u32[]{:S(2)}, u32[]{:S(2)}) collective-permute-start(bf16[2,96,768]{2,1,0:T(8,128)(2,1)S(1)} %slice.400), channel_id=1, source_target_pairs={{0,4},{2,6},{4,0},{6,2},{8,12},{10,14},{12,8},{14,10},{16,20},{18,... | collective-permute-start | bytes 884744 | tf_op jit(solution)/shard_map/ppermute | solution.py:99
  160.2 20.1 %collective-permute-start.40 = (bf16[3,96,768]{2,1,0:T(8,128)(2,1)S(1)}, bf16[3,96,768]{2,1,0:T(8,128)(2,1)}, u32[]{:S(2)}, u32[]{:S(2)}) collective-permute-start(bf16[3,96,768]{2,1,0:T(8,128)(2,1)S(1)} %collective-permute-done.20.refs_16_), channel_id=1, source_target_pairs={{0,2},{2,0},{4,6},{6,4},{8,10},{10,8},{12,14},{14,12},{16,18},{18,... | collective-permute-start | bytes 1327112 | tf_op jit(solution)/shard_map/ppermute | solution.py:99
  175.8 20.5 %collective-permute-start.60 = (bf16[3,96,768]{2,1,0:T(8,128)(2,1)}, bf16[3,96,768]{2,1,0:T(8,128)(2,1)}, u32[]{:S(2)}, u32[]{:S(2)}) collective-permute-start(bf16[3,96,768]{2,1,0:T(8,128)(2,1)} %collective-permute-done.58.refs_15_), channel_id=1, source_target_pairs={{0,1},{1,0},{2,3},{3,2},{4,5},{5,4},{6,7},{7,6},{8,9},{9,8},{10,11... | collective-permute-start | bytes 1327112 | tf_op jit(solution)/shard_map/ppermute | solution.py:99
  177.2 20.5 %collective-permute-start.74 = (bf16[3,96,768]{2,1,0:T(8,128)(2,1)}, bf16[3,96,768]{2,1,0:T(8,128)(2,1)}, u32[]{:S(2)}, u32[]{:S(2)}) collective-permute-start(bf16[3,96,768]{2,1,0:T(8,128)(2,1)} %copy-done.95), channel_id=1, source_target_pairs={{0,2},{2,0},{4,6},{6,4},{8,10},{10,8},{12,14},{14,12},{16,18},{18,... | collective-permute-start | bytes 1327112 | tf_op jit(solution)/shard_map/ppermute | solution.py:99
  182.6 20.5 %collective-permute-start.78 = (bf16[3,96,768]{2,1,0:T(8,128)(2,1)}, bf16[3,96,768]{2,1,0:T(8,128)(2,1)S(1)}, u32[]{:S(2)}, u32[]{:S(2)}) collective-permute-start(bf16[3,96,768]{2,1,0:T(8,128)(2,1)} %collective-permute-done.58.refs_15_), channel_id=1, source_target_pairs={{0,2},{2,0},{4,6},{6,4},{8,10},{10,8},{12,14},{14,12},{16,18},{18,... | collective-permute-start | bytes 1327112 | tf_op jit(solution)/shard_map/ppermute | solution.py:99
  182.7 21.2 %collective-permute-start.61 = (bf16[2,96,768]{2,1,0:T(8,128)(2,1)S(1)}, bf16[2,96,768]{2,1,0:T(8,128)(2,1)}, u32[]{:S(2)}, u32[]{:S(2)}) collective-permute-start(bf16[2,96,768]{2,1,0:T(8,128)(2,1)S(1)} %slice.401), channel_id=1, source_target_pairs={{0,1},{1,0},{2,3},{3,2},{4,5},{5,4},{6,7},{7,6},{8,9},{9,8},{10,11... | collective-permute-start | bytes 884744 | tf_op jit(solution)/shard_map/ppermute | solution.py:99
  211.9 43.1 %collective-permute-start.87 = (bf16[32,768]{1,0:T(8,128)(2,1)S(1)}, bf16[32,768]{1,0:T(8,128)(2,1)S(1)}, u32[]{:S(2)}, u32[]{:S(2)}) collective-permute-start(bf16[32,768]{1,0:T(8,128)(2,1)S(1)} %maximum_select_fusion.1), channel_id=1, source_target_pairs={{0,16},{2,18},{4,20},{6,22},{8,24},{10,26},{12,28},{14,30},{16,0},... | collective-permute-start | bytes 147464 | tf_op jit(solution)/shard_map/ppermute | solution.py:99
  254.8 86.8 %collective-permute-start.131 = (bf16[4,288,768]{2,1,0:T(8,128)(2,1)}, bf16[4,288,768]{2,1,0:T(8,128)(2,1)}, u32[]{:S(2)}, u32[]{:S(2)}) collective-permute-start(bf16[4,288,768]{2,1,0:T(8,128)(2,1)} %bitcast.208), channel_id=1, source_target_pairs={{0,2},{2,0},{4,6},{6,4},{8,10},{10,8},{12,14},{14,12},{16,18},{18,... | collective-permute-start | bytes 5308424 | tf_op jit(solution)/shard_map/ppermute | solution.py:99
  271.8 72.8 %collective-permute-start.127 = (bf16[4,288,768]{2,1,0:T(8,128)(2,1)}, bf16[4,288,768]{2,1,0:T(8,128)(2,1)S(1)}, u32[]{:S(2)}, u32[]{:S(2)}) collective-permute-start(bf16[4,288,768]{2,1,0:T(8,128)(2,1)} %bitcast.18), channel_id=1, source_target_pairs={{0,2},{2,0},{4,6},{6,4},{8,10},{10,8},{12,14},{14,12},{16,18},{18,... | collective-permute-start | bytes 5308424 | tf_op jit(solution)/shard_map/ppermute | solution.py:99
  289.4 62.9 %collective-permute-start.139 = (bf16[4,288,768]{2,1,0:T(8,128)(2,1)}, bf16[4,288,768]{2,1,0:T(8,128)(2,1)S(1)}, u32[]{:S(2)}, u32[]{:S(2)}) collective-permute-start(bf16[4,288,768]{2,1,0:T(8,128)(2,1)} %bitcast.36), channel_id=1, source_target_pairs={{0,2},{2,0},{4,6},{6,4},{8,10},{10,8},{12,14},{14,12},{16,18},{18,... | collective-permute-start | bytes 5308424 | tf_op jit(solution)/shard_map/ppermute | solution.py:99
  299.3 57.3 %collective-permute-start.135 = (bf16[4,288,768]{2,1,0:T(8,128)(2,1)}, bf16[4,288,768]{2,1,0:T(8,128)(2,1)S(1)}, u32[]{:S(2)}, u32[]{:S(2)}) collective-permute-start(bf16[4,288,768]{2,1,0:T(8,128)(2,1)} %bitcast.30), channel_id=1, source_target_pairs={{0,2},{2,0},{4,6},{6,4},{8,10},{10,8},{12,14},{14,12},{16,18},{18,... | collective-permute-start | bytes 5308424 | tf_op jit(solution)/shard_map/ppermute | solution.py:99
  393.7 28.8 %collective-permute-start.155 = (bf16[144,768]{1,0:T(8,128)(2,1)}, bf16[144,768]{1,0:T(8,128)(2,1)}, u32[]{:S(2)}, u32[]{:S(2)}) collective-permute-start(bf16[144,768]{1,0:T(8,128)(2,1)} %get-tuple-element.101), channel_id=1, source_target_pairs={{0,4},{2,6},{4,0},{6,2},{8,12},{10,14},{12,8},{14,10},{16,20},{18,... | collective-permute-start | bytes 663560 | tf_op jit(solution)/shard_map/ppermute | solution.py:99
  398.4 24.9 %collective-permute-start.133 = (bf16[144,768]{1,0:T(8,128)(2,1)}, bf16[144,768]{1,0:T(8,128)(2,1)}, u32[]{:S(2)}, u32[]{:S(2)}) collective-permute-start(bf16[144,768]{1,0:T(8,128)(2,1)} %get-tuple-element.118), channel_id=1, source_target_pairs={{0,4},{2,6},{4,0},{6,2},{8,12},{10,14},{12,8},{14,10},{16,20},{18,... | collective-permute-start | bytes 663560 | tf_op jit(solution)/shard_map/ppermute | solution.py:99
  402.4 21.9 %collective-permute-start.129 = (bf16[144,768]{1,0:T(8,128)(2,1)}, bf16[144,768]{1,0:T(8,128)(2,1)}, u32[]{:S(2)}, u32[]{:S(2)}) collective-permute-start(bf16[144,768]{1,0:T(8,128)(2,1)} %get-tuple-element.112), channel_id=1, source_target_pairs={{0,4},{2,6},{4,0},{6,2},{8,12},{10,14},{12,8},{14,10},{16,20},{18,... | collective-permute-start | bytes 663560 | tf_op jit(solution)/shard_map/ppermute | solution.py:99
  403.5 21.8 %collective-permute-start.141 = (bf16[144,768]{1,0:T(8,128)(2,1)}, bf16[144,768]{1,0:T(8,128)(2,1)}, u32[]{:S(2)}, u32[]{:S(2)}) collective-permute-start(bf16[144,768]{1,0:T(8,128)(2,1)} %get-tuple-element.106), channel_id=1, source_target_pairs={{0,4},{2,6},{4,0},{6,2},{8,12},{10,14},{12,8},{14,10},{16,20},{18,... | collective-permute-start | bytes 663560 | tf_op jit(solution)/shard_map/ppermute | solution.py:99
  405.1 21.2 %collective-permute-start.137 = (bf16[144,768]{1,0:T(8,128)(2,1)}, bf16[144,768]{1,0:T(8,128)(2,1)}, u32[]{:S(2)}, u32[]{:S(2)}) collective-permute-start(bf16[144,768]{1,0:T(8,128)(2,1)} %get-tuple-element.100), channel_id=1, source_target_pairs={{0,4},{2,6},{4,0},{6,2},{8,12},{10,14},{12,8},{14,10},{16,20},{18,... | collective-permute-start | bytes 663560 | tf_op jit(solution)/shard_map/ppermute | solution.py:99
  (276 other events, 4869.6 us)
